TPU v7x, 128 devices: a whole 4x4x4 slice. The times are simulated.
128 devices in a mesh: loader: 8 (over z, core), bucket: 16 (over x, y).
Axes of the slice: x: 4, y: 4, z: 4, core: 2. Of those that a mesh axis runs over, the one named last changes fastest.
Arguments:
- latents: bfloat16 [1024, 512], P(('loader', 'bucket')), may hold values from -6 to 6
- cotangent: bfloat16 [1024, 12288], P(('loader', 'bucket')), may hold values from -6 to 6
- frames: int32 [1024], P(('loader', 'bucket')), may hold values from 1 to 2
- heights: int32 [1024], P(('loader', 'bucket')), may hold values from 1 to 4
- widths: int32 [1024], P(('loader', 'bucket')), may hold values from 1 to 4
- bucket_ids: int32 [1024], P(('loader', 'bucket')), may hold values from 0 to 15, as said below
- w_in: bfloat16 [432, 384], replicated, may hold values from -0.3125 to 0.3125
- w_mid: bfloat16 [10368, 384], replicated, may hold values from -0.0625 to 0.0625
Outputs:
- decoded: bfloat16 [4096, 12288], P(('loader', 'bucket'))
- grad_in: float32 [165888], P(('loader', 'bucket'))
- grad_mid: float32 [3981312], P(('loader', 'bucket'))
Inputs may be any that keep to these rules, and one draw needn't show every extreme that they name: `bucket_ids`: among the tiles of one device at most 2 have one bucket id; in every group along the loader axis one bucket receives exactly 2 tiles from every device of the group.
All inputs are finite; a program needn't handle non-finite values.
Results may differ from a plain program's by a relative error of at most 0.0034.
Values may be sent and summed in bfloat16 or wider, within the bound.
A program may use at most 192 MiB of HBM per device.

v0:
```python
import math

import jax
import jax.numpy as jnp
from jax import lax
from jax.sharding import PartitionSpec as P

Z = 16
C = 384
TAPS = 27
TF = 2
TH = 4
TW = 4
CAP = 2


def tile_mask(frames, heights, widths):
    fpos = jnp.arange(TF)[None, :, None, None]
    rpos = jnp.arange(TH)[None, None, :, None]
    cpos = jnp.arange(TW)[None, None, None, :]
    inside = (
        (fpos < frames[:, None, None, None])
        & (rpos < heights[:, None, None, None])
        & (cpos < widths[:, None, None, None])
    )
    return inside.astype(jnp.float32)[..., None]


def patches(field, flipped):
    if flipped:
        padded = jnp.pad(field, ((0, 0), (0, 2), (1, 1), (1, 1), (0, 0)))
    else:
        padded = jnp.pad(field, ((0, 0), (2, 0), (1, 1), (1, 1), (0, 0)))
    pieces = []
    for first in range(3):
        for second in range(3):
            for third in range(3):
                if flipped:
                    fa, fb, fc = (2 - first, 2 - second, 2 - third)
                else:
                    fa, fb, fc = (first, second, third)
                pieces.append(padded[:, fa : fa + TF, fb : fb + TH, fc : fc + TW, :])
    stacked = jnp.concatenate(pieces, axis=-1)
    return stacked.reshape(-1, stacked.shape[-1])


def decode_tiles(latent_rows, cot_rows, frames, heights, widths, w_in, w_mid):
    count = latent_rows.shape[0]
    mask = tile_mask(frames, heights, widths)
    flat_mask = mask.reshape(-1, 1)
    inputs = (latent_rows.reshape(count, TF, TH, TW, Z).astype(jnp.float32) * mask).astype(
        jnp.bfloat16
    )
    in_patch = patches(inputs, False)
    hidden = jnp.dot(in_patch, w_in, preferred_element_type=jnp.float32)
    scale_rows = lax.rsqrt(jnp.mean(hidden * hidden, axis=-1, keepdims=True) + 1e-06)
    normed = hidden * scale_rows
    sig = jax.nn.sigmoid(normed)
    active = (normed * sig).astype(jnp.bfloat16)
    mid_patch = patches(active.reshape(count, TF, TH, TW, C), False)
    output = hidden + jnp.dot(mid_patch, w_mid, preferred_element_type=jnp.float32)
    decoded_rows = (output * flat_mask).astype(jnp.bfloat16).reshape(count, TF * TH * TW * C)
    grad_out = jnp.where(flat_mask > 0, cot_rows.reshape(-1, C), jnp.zeros((), jnp.bfloat16))
    grad_mid = lax.dot_general(
        mid_patch, grad_out, (((0,), (0,)), ((), ())), preferred_element_type=jnp.float32
    )
    w_flip = jnp.transpose(w_mid.reshape(TAPS, C, C), (0, 2, 1)).reshape(TAPS * C, C)
    back_patch = patches(grad_out.reshape(count, TF, TH, TW, C), True)
    grad_act = jnp.dot(back_patch, w_flip, preferred_element_type=jnp.float32)
    grad_norm = grad_act * sig * (1.0 + normed * (1.0 - sig))
    grad_hidden = grad_out.astype(jnp.float32) + scale_rows * (
        grad_norm - normed * jnp.mean(grad_norm * normed, axis=-1, keepdims=True)
    )
    grad_in = lax.dot_general(
        in_patch,
        grad_hidden.astype(jnp.bfloat16),
        (((0,), (0,)), ((), ())),
        preferred_element_type=jnp.float32,
    )
    return (decoded_rows, grad_in, grad_mid)


def shards(latents, cotangent, frames, heights, widths, bucket_ids, w_in, w_mid):
    owners = lax.axis_size("bucket")
    tiles_total = latents.shape[0] * lax.axis_size("loader") * owners
    onehot = (bucket_ids[:, None] == jnp.arange(owners, dtype=jnp.int32)[None, :]).astype(jnp.int32)
    before = jnp.cumsum(onehot, axis=0) - onehot
    rank = jnp.sum(before * onehot, axis=1)
    slot = bucket_ids * CAP + rank
    slot_ids = jnp.arange(owners * CAP, dtype=jnp.int32)
    placed = slot[None, :] == slot_ids[:, None]
    placer = placed.astype(jnp.bfloat16)
    send_lat = jnp.dot(placer, latents, preferred_element_type=jnp.float32).astype(jnp.bfloat16)
    send_cot = jnp.dot(placer, cotangent, preferred_element_type=jnp.float32).astype(jnp.bfloat16)
    packed = ((frames - 1) * TH + (heights - 1)) * TW + (widths - 1)
    send_code = jnp.sum(placed.astype(jnp.int32) * packed[None, :], axis=1)
    got_lat, got_cot, got_code = (
        lax.all_to_all(send_lat, "bucket", split_axis=0, concat_axis=0, tiled=True),
        lax.all_to_all(send_cot, "bucket", split_axis=0, concat_axis=0, tiled=True),
        lax.all_to_all(send_code, "bucket", split_axis=0, concat_axis=0, tiled=True),
    )
    got_widths = got_code % TW + 1
    got_heights = got_code // TW % TH + 1
    got_frames = got_code // (TW * TH) + 1
    decoded, grad_in, grad_mid = decode_tiles(
        got_lat, got_cot, got_frames, got_heights, got_widths, w_in, w_mid
    )
    summed_in, summed_mid = (
        lax.psum_scatter(
            grad_in.reshape(-1), ("loader", "bucket"), scatter_dimension=0, tiled=True
        ),
        lax.psum_scatter(
            grad_mid.reshape(-1), ("loader", "bucket"), scatter_dimension=0, tiled=True
        ),
    )
    factor = 1.0 / math.sqrt(tiles_total * TF * TH * TW)
    return (decoded, summed_in * factor, summed_mid * factor)


def solution(mesh):
    return jax.shard_map(
        shards,
        mesh=mesh,
        in_specs=(
            P(("loader", "bucket"), None),
            P(("loader", "bucket"), None),
            P(("loader", "bucket")),
            P(("loader", "bucket")),
            P(("loader", "bucket")),
            P(("loader", "bucket")),
            P(),
            P(),
        ),
        out_specs=(P(("loader", "bucket"), None), P(("loader", "bucket")), P(("loader", "bucket"))),
        check_vma=False,
    )
```

profile of v0, /device:TPU:0, one launch (start us, length us, event | category | flops | bytes accessed | tf_op | source)
XLA Modules:
  0.0 552.4 jit_solution(8736679596801235549)
XLA Ops:
  10.3 7.1 %all-to-all-start.1 = ((s32[16,2,1]{1,2,0:T(1,128)}), s32[16,2,1]{1,2,0:T(1,128)S(1)}, u32[]{:S(2)}, u32[]{:S(2)}) async-start(s32[16,2,1]{1,2,0:T(1,128)} %bitcast), calls=%async_computation.1 | async-start | bytes 16384 | tf_op jit(solution)/shard_map/all_to_all | solution.py:100
  40.2 11.5 %copy.19 = bf16[27,384,384]{2,1,0:T(8,128)(2,1)} copy(bf16[27,384,384]{1,2,0:T(8,128)(2,1)} %bitcast.16) | data formatting | bytes 15925248 | tf_op jit(solution)/shard_map/transpose | solution.py:67
  51.7 7.2 %all-to-all-start = ((bf16[16,2,512]{2,1,0:T(2,128)(2,1)}), bf16[16,2,512]{2,1,0:T(2,128)(2,1)S(1)}, u32[]{:S(2)}, u32[]{:S(2)}) async-start(bf16[16,2,512]{2,1,0:T(2,128)(2,1)} %all_to_all.20), calls=%async_computation | async-start | bytes 65536 | tf_op jit(solution)/shard_map/all_to_all | solution.py:98
  60.8 5.7 %all-to-all-done = bf16[16,2,512]{2,1,0:T(2,128)(2,1)S(1)} async-done(((bf16[16,2,512]{2,1,0:T(2,128)(2,1)}), bf16[16,2,512]{2,1,0:T(2,128)(2,1)S(1)}, u32[]{:S(2)}, u32[]{:S(2)}) %all-to-all-start) | async-done | bytes 32800 | tf_op jit(solution)/shard_map/all_to_all | solution.py:98
  66.5 3.6 all-to-all-start.2
  70.9 3.5 pad_slice_fusion.34
  74.5 12.1 %concatenate.79 = bf16[32,2,4,4,432]{4,3,2,1,0:T(4,128)(2,1)S(1)} concatenate(bf16[32,2,4,4,16]{4,3,2,1,0:T(4,128)(2,1)S(1)} %slice.187, bf16[32,2,4,4,16]{4,3,2,1,0:T(4,128)(2,1)S(1)} %slice.187, bf16[32,2,4,4,16]{4,3,2,1,0:T(4,128)(2,1)S(1)} %slice.187, bf16[32,2,4,4,16]{4,3,2,1,0:T(4,128)(2,1)S(1)} %slice.187, bf16[32,2,4,4,16]{4,3,2,1,0:T(4,128)(2,1)S(1)} %slice.187, ...), dimensions={4} | concatenate | bytes 1769472 | tf_op jit(solution)/shard_map/concatenate | solution.py:43
  90.3 6.5 %pad_slice_fusion = (bf16[32,2,4,4,384]{4,3,2,1,0:T(4,128)(2,1)S(1)}, bf16[32,2,4,4,384]{4,3,2,1,0:T(4,128)(2,1)}, bf16[32,2,4,4,384]{4,3,2,1,0:T(4,128)(2,1)}, ...) fusion(bf16[32,2,4,4,384]{4,3,2,1,0:T(4,128)(2,1)S(1)} %broadca, ...), kind=kLoop, calls=%fused_computation | loop fusion | bytes 14155776 | tf_op jit(solution)/shard_map/slice | solution.py:42
  96.8 2.3 concatenate.98
  99.1 2.3 concatenate.99
  101.3 2.3 concatenate.100
  103.6 2.3 concatenate.101
  105.8 2.3 concatenate.102
  108.1 2.3 concatenate.103
  110.4 2.3 concatenate.104
  112.6 2.3 concatenate.105
  114.9 2.3 concatenate.106
  117.2 2.3 concatenate.107
  119.5 2.3 concatenate.108
  121.7 2.3 concatenate.109
  124.0 2.3 concatenate.110
  126.3 2.3 concatenate.111
  128.5 2.3 concatenate.112
  130.8 2.4 concatenate.113
  136.4 2.2 constant_dynamic-update-slice_fusion.34
  138.6 2.2 constant_dynamic-update-slice_fusion.33
  142.9 2.2 constant_dynamic-update-slice_fusion.31
  147.2 2.2 constant_dynamic-update-slice_fusion.29
  149.3 2.2 constant_dynamic-update-slice_fusion.28
  151.5 2.2 constant_dynamic-update-slice_fusion.27
  153.7 2.2 constant_dynamic-update-slice_fusion.26
  155.9 2.2 constant_dynamic-update-slice_fusion.25
  168.4 2.2 constant_dynamic-update-slice_fusion.19
  172.8 19.2 %multiply_reduce_fusion = (f32[1024]{0:T(1024)S(1)}, bf16[1024,384]{1,0:T(8,128)(2,1)S(1)}, f32[1024,384]{1,0:T(8,128)}) fusion(f32[1024,384]{1,0:T(8,128)} %get-tuple-element.64, f32[1024]{0:T(1024)S(1)} %add_rsqrt_fusion, bf16[1024,10368]{1,0:T(8,128)(2,1)} %constant_dynamic-update-slice_fusion.18, bf16[10368,384]{1,0:T(8,128)(2,1)} %bitcast.17), kind=kOutput, calls=%fused_computation.55 | convolution fusion | flops 8158837760 | bytes 33136640 | tf_op jit(solution)/shard_map/dot_general | solution.py:69
  193.9 12.3 %pad_slice_fusion.17 = (bf16[32,2,4,4,384]{4,3,2,1,0:T(4,128)(2,1)S(1)}, bf16[32,2,4,4,384]{4,3,2,1,0:T(4,128)(2,1)}, bf16[32,2,4,4,384]{4,3,2,1,0:T(4,128)(2,1)...) fusion(bf16[32,2,4,4,384]{4,3,2,1,0:T(4,128)(2,1)} %reshape.318), kind=kLoop, calls=%fused_computation.17 | loop fusion | bytes 14155776 | tf_op jit(solution)/shard_map/slice | solution.py:42
  206.2 2.3 concatenate.80
  208.5 2.3 concatenate.81
  210.7 2.3 concatenate.82
  213.0 2.3 concatenate.83
  215.3 2.3 concatenate.84
  217.5 2.5 concatenate.85
  220.0 2.3 concatenate.86
  222.3 2.3 concatenate.87
  224.6 2.3 concatenate.88
  226.8 2.3 concatenate.89
  229.1 2.3 concatenate.90
  231.4 2.3 concatenate.91
  233.7 2.3 concatenate.92
  238.1 2.2 constant_dynamic-update-slice_fusion.16
  242.3 2.2 constant_dynamic-update-slice_fusion.14
  246.6 2.2 constant_dynamic-update-slice_fusion.12
  248.8 2.1 constant_dynamic-update-slice_fusion.11
  253.1 2.2 constant_dynamic-update-slice_fusion.9
  259.5 2.2 constant_dynamic-update-slice_fusion.6
  265.9 2.3 concatenate.93
  268.2 2.3 concatenate.94
  270.4 2.3 concatenate.95
  273.8 2.2 constant_dynamic-update-slice_fusion.3
  278.1 2.2 constant_dynamic-update-slice_fusion.1
  282.4 19.2 %fusion.11 = f32[10368,384]{1,0:T(8,128)} fusion(bf16[1024,10368]{1,0:T(8,128)(2,1)} %constant_dynamic-update-slice_fusion, bf16[1024,384]{1,0:T(8,128)(2,1)S(1)} %reshape.320, pred[1024]{0:T(1024)(128)(4,1)S(1)} %broadcast_compare_fusion.1), kind=kOutput, calls=%fused_computation.157 | convolution fusion | flops 8154120192 | bytes 37946368 | tf_op jit(solution)/shard_map/dot_general | solution.py:64
  301.6 17.3 %reshape.325 = f32[3981312]{0:T(1024)} reshape(f32[10368,384]{1,0:T(8,128)} %fusion.11) | data formatting | bytes 31850496 | tf_op jit(solution)/shard_map/reshape | solution.py:113
  318.9 2.9 fusion.1
  322.7 17.9 %multiply_convert_fusion = bf16[1024,384]{1,0:T(8,128)(2,1)S(1)} fusion(f32[1024,384]{1,0:T(8,128)} %get-tuple-element.64, bf16[1024,10368]{1,0:T(8,128)(2,1)} %constant_dynamic-update-slice_fusion, bf16[10368,384]{1,0:T(8,128)(2,1)} %param.15, f32[1024]{0:T(1024)S(1)} %reshape.327), kind=kOutput, calls=%fused_computation.56 | convolution fusion | flops 8154906624 | bytes 31559680 | tf_op jit(solution)/shard_map/dot_general | solution.py:61
  341.9 200.4 %all-reduce.8.cloned.1.call-done = (f32[165888]{0:T(1024)}, f32[3981312]{0:T(1024)}) async-done(((f32[165888]{0:T(1024)}, f32[3981312]{0:T(1024)}), (f32[165888]{0:T(1024)}, f32[3981312]{0:T(1024)})) %all-reduce.8.cloned.1.call-update) | async-done | bytes 16588816
  (85 shorter events, 81.9 us)
Async XLA Ops:
  7.2 80.0 %copy-start = (bf16[432,384]{1,0:T(8,128)(2,1)S(1)}, bf16[432,384]{1,0:T(8,128)(2,1)}, u32[]{:S(2)}) copy-start(bf16[432,384]{1,0:T(8,128)(2,1)} %param.14) | copy-start | bytes 995332
  10.3 41.4 %all-to-all-start.1 = ((s32[16,2,1]{1,2,0:T(1,128)}), s32[16,2,1]{1,2,0:T(1,128)S(1)}, u32[]{:S(2)}, u32[]{:S(2)}) async-start(s32[16,2,1]{1,2,0:T(1,128)} %bitcast), calls=%async_computation.1 | async-start | bytes 16384 | tf_op jit(solution)/shard_map/all_to_all | solution.py:100
  51.7 14.9 %all-to-all-start = ((bf16[16,2,512]{2,1,0:T(2,128)(2,1)}), bf16[16,2,512]{2,1,0:T(2,128)(2,1)S(1)}, u32[]{:S(2)}, u32[]{:S(2)}) async-start(bf16[16,2,512]{2,1,0:T(2,128)(2,1)} %all_to_all.20), calls=%async_computation | async-start | bytes 65536 | tf_op jit(solution)/shard_map/all_to_all | solution.py:98
  66.5 22.6 %all-to-all-start.2 = ((bf16[16,2,12288]{2,1,0:T(2,128)(2,1)}), bf16[16,2,12288]{2,1,0:T(2,128)(2,1)S(1)}, u32[]{:S(2)}, u32[]{:S(2)}) async-start(bf16[16,2,12288]{2,1,0:T(2,128)(2,1)} %all_to_all.25), calls=%async_computation.2 | async-start | bytes 1572864 | tf_op jit(solution)/shard_map/all_to_all | solution.py:99
  70.1 472.2 %all-reduce.8.cloned.1.call-start = ((), (), s32[]{:S(2)}) async-start(), calls=%async_computation.3 | async-start | bytes 33177600
  192.0 0.9 copy-start.2
  322.7 222.6 %copy-start.1 = (bf16[432,384]{1,0:T(8,128)(2,1)S(1)}, bf16[432,384]{1,0:T(8,128)(2,1)}, u32[]{:S(2)}) copy-start(bf16[432,384]{1,0:T(8,128)(2,1)} %param.14) | copy-start | bytes 995332
Sparse Core Ops, SparseCore 0:
  322.8 219.4 all-reduce.7
where the time goes:
time: 561 us; the launch traced here: 552 us
  local copies, waits for them, and re-layouts  242 us (43%)
  waiting for transfers between devices  206 us (37%)
  matrix products  63.4 us (11%)
  starting transfers between devices  18 us (3%)
  between operations  14.5 us (3%)
  other arithmetic  8.85 us (2%)
    unnamed x2, waiting for transfers between devices  200 us
    concatenate x37, local copies, waits for them, and re-layouts, patches(): stacked = jnp.concatenate(pieces, axis=-1)  91.4 us
    unnamed x57, local copies, waits for them, and re-layouts  90.3 us
    slice x4, local copies, waits for them, and re-layouts, patches(): pieces.append(padded[:, fa:fa + TF, fb:fb + TH, fc:fc + TW, :])  22.3 us
    dot_general x1, matrix products, decode_tiles(): grad_act = jnp.dot(back_patch, w_flip, preferred_element_type=jnp.float32)  19.2 us
    dot_general x1, matrix products, decode_tiles(): lax.dot_general(mid_patch, grad_out, (((0,), (0,)), ((), ())), preferred_...  19.2 us
    dot_general x1, matrix products, decode_tiles(): jnp.dot(mid_patch, w_mid, preferred_element_type=jnp.float32)  17.9 us
    reshape x1, local copies, waits for them, and re-layouts, shards(): grad_mid.reshape(-1)  17.3 us
  transfers between devices with their start and end apart: 4, of which 2 were waited for; matrix products, arithmetic and copies ran while one was open for 13% of the time, Pallas kernels for 0%

commit v1 on v0

v1 whole, which is shorter than its diff:
```python
import math

import jax
import jax.numpy as jnp
from jax import lax
from jax.experimental import pallas as pl
from jax.experimental.pallas import tpu as pltpu
from jax.sharding import PartitionSpec as P

Z = 16
C = 384
TAPS = 27
TF = 2
TH = 4
TW = 4
CAP = 2
EPS = 1e-06
BF = jnp.bfloat16
F32 = jnp.float32
MESH = pl.DeviceIdType.MESH
ORDERS = (("z", "x", "y"), ("x", "y", "z"), ("y", "z", "x"))
ROWS = 1296
PIECE = 96
GROWS = 80


def al(v, m):
    return pl.multiple_of(v, m)


def kernel(
    xs_ref, snd_ref, cot_ref, mask_ref, win_ref, wmid_ref,
    dec_ref, gin_ref, gmid_ref,
    w, we, rcv, xsp, xbf, xbp, hf, uef, ut, gyef, gyep, gua, ghs, df, gif, gib, rgi, gz, gzb, rz, gx, gxb, rx,
    gyv, gyb, ry, g, rc, s1, p1, fl1, fr1, s2f, s2, p2, fl2, fr2, s3, p3, fl3, fr3, ud, acc,
    w_sem, a_send, a_recv, c_send, c_recv, r_send, r_recv, i_send, i_recv,
):
    load = lax.axis_index("loader")
    q = lax.axis_index("bucket")
    z, c = load // 2, load % 2
    x, y = q // 4, q % 4
    pos = {"z": z, "x": x, "y": y}
    sib = (z * 2 + (1 - c), q)

    def dev(axis, v):
        if axis == "z":
            return (v * 2 + c, q)
        if axis == "x":
            return (load, v * 4 + y)
        return (load, x * 4 + v)

    def wcopy(i):
        part = pl.ds(i * 1152, 1152)
        return pltpu.make_async_copy(wmid_ref.at[part], w.at[part], w_sem.at[i])

    for i in range(9):
        wcopy(i).start()

    barrier = pltpu.get_barrier_semaphore()

    @pl.loop(1, 16)
    def _(d):
        pl.semaphore_signal(barrier, 1, device_id=(load, lax.rem(q + d, 16)), device_id_type=MESH)

    for d in range(1, 4):
        pl.semaphore_signal(barrier, 1, device_id=dev("z", lax.rem(z + d, 4)), device_id_type=MESH)
    pl.semaphore_signal(barrier, 1, device_id=sib, device_id_type=MESH)
    pl.semaphore_wait(barrier, 19)

    def acopy(d):
        to = lax.rem(q + d, 16)
        return pltpu.make_async_remote_copy(
            snd_ref.at[to], rcv.at[q], a_send.at[d], a_recv.at[d], device_id=(load, to), device_id_type=MESH)

    def afrom(d):
        src = lax.rem(q - d + 16, 16)
        return pltpu.make_async_remote_copy(
            snd_ref.at[src], rcv.at[src], a_send.at[d], a_recv.at[d], device_id=(load, src), device_id_type=MESH)

    @pl.loop(1, 16)
    def _(d):
        acopy(d).start()

    rcv[q] = snd_ref[q]

    we[...] = jnp.zeros_like(we)
    for a in range(3):
        for b in range(3):
            for cc in range(4):
                for e in range(3):
                    ci = cc + e - 1
                    if 0 <= ci < 4:
                        we[a * 256 + (b * 4 + ci) * 16 : a * 256 + (b * 4 + ci) * 16 + 16, cc * C : cc * C + C] = (
                            win_ref[(a * 9 + b * 3 + e) * 16 : (a * 9 + b * 3 + e) * 16 + 16, :])

    xsp[0:64, :] = jnp.zeros((64, 256), BF)
    xsp[64:128, :] = xs_ref[...].astype(BF)
    h = jnp.dot(xsp[0:64, :], we[0:256, :], preferred_element_type=F32)
    h += jnp.dot(xsp[32:96, :], we[256:512, :], preferred_element_type=F32)
    h += jnp.dot(xsp[64:128, :], we[512:768, :], preferred_element_type=F32)
    for fr in range(8):
        for cc in range(4):
            hf[(fr * 4 + cc) * 8 : (fr * 4 + cc) * 8 + 8, :] = h[fr * 8 : fr * 8 + 8, cc * C : cc * C + C]

    def act(hv):
        rr = lax.rsqrt(jnp.mean(hv * hv, axis=-1, keepdims=True) + EPS)
        gv = hv * rr
        sg = jax.nn.sigmoid(gv)
        return rr, gv, sg

    hv = hf[...]
    rr, gn, sg = act(hv)
    u = gn * sg
    uef[...] = jnp.zeros_like(uef)
    gyef[...] = jnp.zeros_like(gyef)
    uef[:, C : 2 * C] = u
    cot = cot_ref[...].astype(F32)
    for p in range(32):
        gyef[p * 8 : p * 8 + 8, C : 2 * C] = jnp.where(
            mask_ref[:, p : p + 1] > 0, cot[:, p * C : p * C + C], 0.0)
    for fr in range(8):
        lo, hi = slice(fr * 32, fr * 32 + 24), slice(fr * 32 + 8, fr * 32 + 32)
        uef[hi, 0:C] = uef[lo, C : 2 * C]
        uef[lo, 2 * C : 3 * C] = uef[hi, C : 2 * C]
        gyef[lo, 0:C] = gyef[hi, C : 2 * C]
        gyef[hi, 2 * C : 3 * C] = gyef[lo, C : 2 * C]
    ut[...] = uef[...].T.astype(BF)
    gyep[...] = jnp.zeros_like(gyep)
    for f in range(2):
        gyep[(f * 6 + 1) * 32 : (f * 6 + 5) * 32, :] = gyef[f * 128 : f * 128 + 128, :].astype(BF)

    def ccopy(zz):
        return pltpu.make_async_remote_copy(
            g.at[pl.ds(al((zz * 2 + 1 - c) * ROWS, 16), ROWS)], rc.at[zz], c_send.at[zz], c_recv.at[zz],
            device_id=sib, device_id_type=MESH)

    def shifted(i, lanes):
        a, b = i // 3, i % 3
        o0 = al(((2 - a) * 6 + 2 - b) * 32, 32)
        o1 = al(((3 - a) * 6 + 2 - b) * 32, 32)
        return jnp.concatenate([gyep[pl.ds(o0, 128), lanes], gyep[pl.ds(o1, 128), lanes]], axis=0)

    @pl.loop(0, 9)
    def _(i):
        rhs = shifted(i, slice(C, 2 * C))
        g[pl.ds(al(i * 1152, 16), 1152), :] = jnp.dot(ut[...], rhs, preferred_element_type=F32).astype(BF)
        ready = i - 1

        @pl.when((i >= 1) & (lax.rem(ready + 2, 2) != c))
        def _():
            ccopy(ready // 2).start()

    def place(j, zz, xx, yy):
        at = {"z": zz, "x": xx, "y": yy}
        i1, i2, i3 = (at[n] for n in ORDERS[j])
        return j * 64 + i1 * 16 + i2 * 4 + i3

    for zz in range(4):
        ccopy(zz).wait_recv()

        @pl.loop(0, 16)
        def _(k):
            own = al((zz * 2 + c) * ROWS + k * 80, 16)
            other = al(k * 80, 16)
            for j in range(3):
                lanes = slice(j * 128, j * 128 + 128)
                s1[place(j, zz, k // 4, k % 4)] = (
                    g[pl.ds(own, PIECE), lanes].astype(F32) + rc[zz, pl.ds(other, PIECE), lanes].astype(F32)).astype(BF)

    def half1(j, t, h):
        return s1.at[pl.ds(j * 64 + t * 16 + h * 8, 8)]

    def half2(j, t, h):
        return s2.at[pl.ds(j * 16 + t * 4 + h * 2, 2)]

    def half3(j, t, h):
        return s3.at[j * 4 + t, h * 48 : h * 48 + 48]

    def from1(ref, j, h):
        return ref.at[pl.ds(j * 16 + h * 8, 8)]

    def from2(ref, j, h):
        return ref.at[pl.ds(j * 4 + h * 2, 2)]

    def from3(ref, j, h):
        return ref.at[j, h * 48 : h * 48 + 48]

    stages = ((half1, p1, fl1, fr1, from1), (half2, p2, fl2, fr2, from2), (half3, p3, fl3, fr3, from3))

    def ring(j, st, n):
        half, part, fl, fr, into = stages[st]
        axis = ORDERS[j][st]
        me = pos[axis]
        right, left, far = lax.rem(me + 1, 4), lax.rem(me + 3, 4), lax.rem(me + 2, 4)
        src, to, dst = (
            (half(j, far, 0), right, part.at[j * 2]),
            (half(j, far, 1), left, part.at[j * 2 + 1]),
            (half(j, right, 1), right, into(fl, j, 1)),
            (half(j, left, 0), left, into(fr, j, 0)),
            (half(j, right, 0), right, into(fl, j, 0)),
            (half(j, left, 1), left, into(fr, j, 1)),
        )[n]
        k = (j * 3 + st) * 6 + n
        return pltpu.make_async_remote_copy(
            src, dst, r_send.at[k], r_recv.at[k], device_id=dev(axis, to), device_id_type=MESH)

    def begin(st):
        for n in range(4):
            for j in range(3):
                ring(j, st, n).start()

    def relay(st):
        half, part = stages[st][0], stages[st][1]
        for n in range(2):
            for j in range(3):
                me = pos[ORDERS[j][st]]
                ring(j, st, n).wait_recv()
                ref = half(j, lax.rem(me + (1 if n == 0 else 3), 4), n)
                ref[...] = (ref[...].astype(F32) + part[j * 2 + n].astype(F32)).astype(ref.dtype)
                ring(j, st, 4 + n).start()

    def arrived(st):
        for j in range(3):
            for n in range(2, 6):
                ring(j, st, n).wait_recv()

    def finish1():
        arrived(0)
        for j in range(3):

            @pl.loop(0, 16)
            def _(k):
                at = {ORDERS[j][0]: pos[ORDERS[j][0]], ORDERS[j][1]: k // 4, ORDERS[j][2]: k % 4}
                off = (at["x"] * 4 + at["y"]) * 80
                lanes = slice(j * 128, j * 128 + 128)
                total = (
                    g[pl.ds(al((at["z"] * 2 + c) * ROWS + off, 16), PIECE), lanes].astype(F32)
                    + rc[at["z"], pl.ds(al(off, 16), PIECE), lanes].astype(F32)
                    + fl1[j * 16 + k].astype(F32) + fr1[j * 16 + k].astype(F32))
                s2f[j * 16 + k] = total
                s2[j * 16 + k] = total.astype(BF)

    def finish2():
        arrived(1)
        for j in range(3):
            me = pos[ORDERS[j][1]]
            for k in range(4):
                s3[j * 4 + k] = s2f[j * 16 + me * 4 + k] + fl2[j * 4 + k].astype(F32) + fr2[j * 4 + k].astype(F32)

    def finish3():
        arrived(2)
        for j in range(3):
            gmid_ref[:, j * 128 : j * 128 + 128] = s3[j * 4 + pos[ORDERS[j][2]]] + fl3[j] + fr3[j]

    begin(0)

    for i in range(9):
        wcopy(i).wait()
    gua[...] = jnp.zeros_like(gua)

    @pl.loop(0, 9)
    def _(i):
        total = gua[...]
        for e in range(3):
            lhs = shifted(i, slice(e * C, e * C + C))
            wk = w[pl.ds(al(i * 1152 + e * C, 16), C), :]
            total += lax.dot_general(lhs, wk, (((1,), (1,)), ((), ())), preferred_element_type=F32)
        gua[...] = total

    rr, gn, sg = act(hf[...])
    gv = gua[...] * sg * (1.0 + gn * (1.0 - sg))
    gh = gyef[:, C : 2 * C] + rr * (gv - gn * jnp.mean(gv * gn, axis=-1, keepdims=True))
    hf[...] = gh
    ghs[...] = jnp.zeros_like(ghs)
    for cc in range(4):
        ghs[0:64, cc * C : cc * C + C] = jnp.concatenate(
            [hf[(fr * 4 + cc) * 8 : (fr * 4 + cc) * 8 + 8, :] for fr in range(8)], axis=0).astype(BF)
    xst = xs_ref[...].T.astype(BF)
    gif[...] = jnp.zeros_like(gif)
    for a in range(3):
        df[...] = jnp.dot(xst, ghs[(2 - a) * 32 : (2 - a) * 32 + 64, :], preferred_element_type=F32)
        for b in range(3):
            for e in range(3):
                total = jnp.zeros((16, C), F32)
                for cc in range(4):
                    ci = cc + e - 1
                    if 0 <= ci < 4:
                        total += df[(b * 4 + ci) * 16 : (b * 4 + ci) * 16 + 16, cc * C : cc * C + C]
                gif[(a * 9 + b * 3 + e) * 16 : (a * 9 + b * 3 + e) * 16 + 16, :] = total
    for blk in range(8):
        at = 16 * ((27 * blk) // 8)
        gib[blk % 2, blk // 2] = gif[at : at + GROWS, :].astype(BF)

    def icore():
        return pltpu.make_async_remote_copy(
            gib.at[1 - c], rgi, i_send.at[0], i_recv.at[0], device_id=sib, device_id_type=MESH)

    base = load * 54 - 16 * ((27 * load) // 8)

    def xstart(v):
        return al(16 * ((2 * base + 27 * v) // 32), 16)

    def ipeer(axis, d):
        v = lax.rem(pos[axis] + d, 4)
        src, dst, k = {
            "z": (gzb.at[v], rz.at[d - 1], 0),
            "x": (gxb.at[pl.ds(xstart(v), 32)], rx.at[d - 1], 3),
            "y": (gyb, ry.at[d - 1], 6),
        }[axis]
        return pltpu.make_async_remote_copy(
            src, dst, i_send.at[k + d], i_recv.at[k + d], device_id=dev(axis, v), device_id_type=MESH)

    def in_z():
        icore().wait_recv()
        for zz in range(4):
            at = al(16 * ((27 * (zz * 2 + c)) // 8), 16)
            total = gif[pl.ds(at, GROWS), :] + rgi[zz].astype(F32)
            gz[zz] = total
            gzb[zz] = total.astype(BF)
        for d in range(1, 4):
            ipeer("z", d).start()

    def in_x():
        for d in range(1, 4):
            ipeer("z", d).wait_recv()
        total = gz[z] + rz[0].astype(F32) + rz[1].astype(F32) + rz[2].astype(F32)
        gx[...] = total
        gxb[...] = total.astype(BF)
        for d in range(1, 4):
            ipeer("x", d).start()

    def in_y():
        for d in range(1, 4):
            ipeer("x", d).wait_recv()
        total = gx[pl.ds(xstart(x), 32), :] + rx[0].astype(F32) + rx[1].astype(F32) + rx[2].astype(F32)
        gyv[...] = total
        gyb[...] = total.astype(BF)
        for d in range(1, 4):
            ipeer("y", d).start()

    def in_end():
        for d in range(1, 4):
            ipeer("y", d).wait_recv()
        gin_ref[...] = gyv[...] + ry[0].astype(F32) + ry[1].astype(F32) + ry[2].astype(F32)

    icore().start()
    relay(0)

    @pl.loop(1, 16)
    def _(d):
        afrom(d).wait_recv()

    for fr in range(8):
        for j in range(2):
            for n in range(2):
                xbf[n, pl.ds(fr * 32 + j, 16, stride=2), :] = rcv[:, fr, j * 256 + n * 128 : j * 256 + n * 128 + 128]
    xbp[0:256, :] = jnp.zeros((256, 256), BF)
    xbp[256:512, 0:128] = xbf[0].astype(BF)
    xbp[256:512, 128:256] = xbf[1].astype(BF)
    ud[...] = jnp.zeros_like(ud)
    for f in range(2):
        hd = jnp.dot(xbp[f * 128 : f * 128 + 128, :], we[0:256, :], preferred_element_type=F32)
        hd += jnp.dot(xbp[f * 128 + 128 : f * 128 + 256, :], we[256:512, :], preferred_element_type=F32)
        hd += jnp.dot(xbp[f * 128 + 256 : f * 128 + 384, :], we[512:768, :], preferred_element_type=F32)
        for cc in range(4):
            hc = hd[:, cc * C : cc * C + C]
            _, gc, sc = act(hc)
            uc = (gc * sc).astype(BF)
            for r in range(4):
                rows = slice(r * 32, r * 32 + 32)
                acc[((f * 4 + r) * 4 + cc) * 32 : ((f * 4 + r) * 4 + cc) * 32 + 32, :] = hc[rows]
                to = ((f + 2) * 6 + r + 1) * 128 + cc * 32
                for e in range(3):
                    if 0 <= cc - e + 1 < 4:
                        ud[to + (1 - e) * 32 : to + (1 - e) * 32 + 32, e * C : e * C + C] = uc[rows]

    def second():
        finish1()
        begin(1)

    def third():
        finish2()
        begin(2)

    events = {
        0: in_z, 3: in_x, 6: in_y, 9: in_end,
        10: second, 12: lambda: relay(1), 14: third, 15: lambda: relay(2),
    }

    @pl.loop(0, 18)
    def _(s):
        f, i = s // 9, lax.rem(s, 9)
        a, b = i // 3, lax.rem(i, 3)
        lhs = ud[pl.ds(al(((f + a) * 6 + b) * 128, 128), 512), :]
        rows = pl.ds(al(f * 512, 512), 512)
        acc[rows, :] += jnp.dot(lhs, w[pl.ds(al(i * 1152, 16), 1152), :], preferred_element_type=F32)
        for at, event in events.items():
            pl.when(s == at)(event)

    for fr in range(8):
        for cc in range(4):
            p = fr * 4 + cc
            m = xbf[1, fr * 32 : fr * 32 + 32, 64 + cc : 65 + cc]
            dec_ref[:, p * C : p * C + C] = (acc[p * 32 : p * 32 + 32, :] * m).astype(BF)
    finish3()

    @pl.loop(1, 16)
    def _(d):
        acopy(d).wait_send()

    for zz in range(4):
        ccopy(zz).wait_send()
    for st in range(3):
        for j in range(3):
            for n in range(6):
                ring(j, st, n).wait_send()
    icore().wait_send()
    for axis in ("z", "x", "y"):
        for d in range(1, 4):
            ipeer(axis, d).wait_send()


def tile_mask(frames, heights, widths):
    fpos = jnp.arange(TF)[None, :, None, None]
    rpos = jnp.arange(TH)[None, None, :, None]
    cpos = jnp.arange(TW)[None, None, None, :]
    inside = (
        (fpos < frames[:, None, None, None])
        & (rpos < heights[:, None, None, None])
        & (cpos < widths[:, None, None, None])
    )
    return inside.astype(F32)


def shards(latents, cotangent, frames, heights, widths, bucket_ids, w_in, w_mid):
    owners = lax.axis_size("bucket")
    count = latents.shape[0]
    tiles_total = count * lax.axis_size("loader") * owners
    mask = tile_mask(frames, heights, widths)
    xm = latents.reshape(count, TF, TH, TW, Z).astype(F32) * mask[..., None]
    xm = jnp.pad(xm.reshape(count, TF, TH, TW * Z), ((0, 0), (0, 0), (1, 1), (0, 0)))
    xb = jnp.concatenate(
        [xm[:, :, 0:4], xm[:, :, 1:5], xm[:, :, 2:6], mask, jnp.zeros((count, TF, TH, 60), F32)], axis=-1
    ).reshape(count, 8, 256)
    same = bucket_ids[:, None] == bucket_ids[None, :]
    rank = jnp.sum(jnp.tril(same, -1).astype(jnp.int32), axis=1)
    slot = bucket_ids * CAP + rank
    placer = (slot[None, :] == jnp.arange(owners * CAP, dtype=jnp.int32)[:, None]).astype(F32)
    snd = jnp.dot(placer, xb.reshape(count, 2048), preferred_element_type=F32)
    snd = snd.reshape(owners, CAP, 8, 256).transpose(0, 2, 1, 3).reshape(owners, 8, 512)
    xs = xb.transpose(1, 0, 2).reshape(64, 256)

    v = pltpu.VMEM
    dma = pltpu.SemaphoreType.DMA
    vm = pl.BlockSpec(memory_space=pltpu.VMEM)
    dec, gin, gmid = pl.pallas_call(
        kernel,
        out_shape=(
            jax.ShapeDtypeStruct((32, 12288), BF),
            jax.ShapeDtypeStruct((32, C), F32),
            jax.ShapeDtypeStruct((PIECE, C), F32),
        ),
        in_specs=[vm, vm, vm, vm, vm, pl.BlockSpec(memory_space=pl.ANY)],
        out_specs=(vm, vm, vm),
        scratch_shapes=[
            v((10368, C), BF), v((768, 1536), BF), v((16, 8, 512), F32), v((128, 256), BF), v((2, 256, 128), F32),
            v((512, 256), BF), v((256, C), F32), v((256, 1152), F32), v((1152, 256), BF), v((256, 1152), F32),
            v((768, 1152), BF), v((256, C), F32), v((128, 1536), BF), v((256, 1536), F32), v((448, C), F32),
            v((2, 4, GROWS, C), BF), v((4, GROWS, C), BF), v((4, GROWS, C), F32), v((4, GROWS, C), BF),
            v((3, GROWS, C), BF), v((GROWS, C), F32), v((GROWS, C), BF), v((3, 32, C), BF),
            v((32, C), F32), v((32, C), BF), v((3, 32, C), BF), v((10368, C), BF), v((4, ROWS, C), BF),
            v((192, PIECE, 128), BF), v((6, 8, PIECE, 128), BF), v((48, PIECE, 128), BF), v((48, PIECE, 128), BF),
            v((48, PIECE, 128), F32), v((48, PIECE, 128), BF), v((6, 2, PIECE, 128), BF), v((12, PIECE, 128), BF),
            v((12, PIECE, 128), BF), v((12, PIECE, 128), F32), v((6, 48, 128), F32), v((3, PIECE, 128), F32),
            v((3, PIECE, 128), F32), v((3072, 1152), BF), v((1024, C), F32),
            dma((9,)), dma((16,)), dma((16,)), dma((4,)), dma((4,)), dma((54,)), dma((54,)), dma((10,)), dma((10,)),
        ],
        compiler_params=pltpu.CompilerParams(
            collective_id=0, has_side_effects=True, vmem_limit_bytes=62 * 1024 * 1024),
    )(xs, snd, cotangent, mask.reshape(count, 32), w_in, w_mid)

    factor = 1.0 / math.sqrt(tiles_total * TF * TH * TW)
    load = lax.axis_index("loader")
    q = lax.axis_index("bucket")
    base = load * 54 - 16 * ((27 * load) // 8)
    start = 16 * ((2 * base + 27 * (q // 4)) // 32)
    grad_in = lax.dynamic_slice(gin.reshape(-1), (384 * (base - start) + 1296 * q,), (1296,)) * factor
    grad_mid = lax.dynamic_slice(gmid, (q, 0), (81, C)).reshape(-1) * factor
    return (dec, grad_in, grad_mid)


def solution(mesh):
    return jax.shard_map(
        shards,
        mesh=mesh,
        in_specs=(
            P(("loader", "bucket"), None),
            P(("loader", "bucket"), None),
            P(("loader", "bucket")),
            P(("loader", "bucket")),
            P(("loader", "bucket")),
            P(("loader", "bucket")),
            P(),
            P(),
        ),
        out_specs=(P(("loader", "bucket"), None), P(("loader", "bucket")), P(("loader", "bucket"))),
        check_vma=False,
    )
```

time: 561 us -> 77.3 us (0.14); the launches traced: 552 us -> 76.9 us
  local copies, waits for them, and re-layouts: 242 us -> 8.27 us
  waiting for transfers between devices: 206 us -> 0 us
  matrix products: 63.4 us -> 0.29 us
  Pallas kernels: 0 us -> 62.3 us
  starting transfers between devices: 18 us -> 0 us
  between operations: 14.5 us -> 0.79 us
    unnamed x2 -> x0, waiting for transfers between devices: 200 us -> none
    concatenate x37 -> x2, local copies, waits for them, and re-layouts: 91.4 us -> 0.88 us  [shards(): jnp.concatenate([xm[:, :, 0:4], xm[:, :, 1:5], xm[:, :, 2:6], mask, jnp.z...]
    unnamed x57 -> x1, local copies, waits for them, and re-layouts: 90.3 us -> 2.06 us
    dot_general x7 -> x1, matrix products: 63.4 us -> 0.29 us  [shards(): snd = jnp.dot(placer, xb.reshape(count, 2048), preferred_element_type=F32)]
    pallas_call x0 -> x1, Pallas kernels: none -> 62.3 us  [shards(): pl.pallas_call(kernel, out_shape=(jax.ShapeDtypeStruct((32, 12288), BF),...]
    slice x4 -> x3, local copies, waits for them, and re-layouts: 22.3 us -> 0.04 us  [the longest x2 0.03 us: shards(): xm[:, :, 2:6]]
    reshape x7 -> x1, local copies, waits for them, and re-layouts: 22.2 us -> 0.8 us  [shards(): gin.reshape(-1)]
    all_to_all x3 -> x0, starting transfers between devices: 18 us -> none  [the longest x1 7.22 us: shards(): lax.all_to_all(send_lat, 'bucket', split_axis=0, concat_axis=0, tiled=True)]
  transfers between devices with their start and end apart: 4 -> 0, of which waited for: 2 -> 0; matrix products, arithmetic and copies ran while one was open for 13% -> 0% of each run, Pallas kernels for 0% -> 0%
where the time goes in v1:
time: 77.3 us; the launch traced here: 76.9 us
  Pallas kernels  62.3 us (81%)
  local copies, waits for them, and re-layouts  8.27 us (11%)
  other arithmetic  5.29 us (7%)
  between operations  0.79 us (1%)
    pallas_call x1, Pallas kernels, shards(): pl.pallas_call(kernel, out_shape=(jax.ShapeDtypeStruct((32, 12288), BF),...  62.3 us
    unnamed x1, local copies, waits for them, and re-layouts  2.06 us
    convert_element_type x2, local copies, waits for them, and re-layouts, shards(): xm = latents.reshape(count, TF, TH, TW, Z).astype(F32) * mask[..., None]  1.56 us

profile of v1, /device:TPU:0, one launch (start us, length us, event | category | flops | bytes accessed | tf_op | source)
XLA Modules:
  0.0 76.9 jit_solution(16570392362882129006)
XLA Ops:
  0.7 0.7 iota_compare_fusion.2
  1.4 0.7 iota_compare_fusion.3
  2.0 0.7 iota_compare_fusion.1
  2.7 0.1 copy.27
  2.8 0.1 mul.52
  3.0 0.1 reshape.154
  3.1 0.8 %reshape.149 = f32[8,2,4,64]{3,2,1,0:T(4,128)S(1)} reshape(bf16[8,512]{1,0:T(8,128)(2,1)} %param.8) | data formatting | bytes 24576 | tf_op jit(solution)/shard_map/convert_element_type | solution.py:440
  3.9 0.1 copy.33
  4.1 0.2 concatenate.13
  4.3 0.9 %convert_reduce_fusion = s32[8]{0:T(128)S(1)} fusion(s32[8]{0:T(128)} %param.13, s32[8]{0:T(128)S(1)} %iota_add_fusion), kind=kLoop, calls=%fused_computation.12 | loop fusion | flops 312 | bytes 96 | tf_op jit(solution)/shard_map/reduce_sum | solution.py:446
  5.2 0.7 multiply_add_fusion.1
  5.8 0.3 convolution_bitcast_fusion
  6.1 0.9 %copy.34 = f32[16,8,2,256]{3,1,2,0:T(8,128)} copy(f32[16,8,2,256]{3,0,1,2:T(8,128)S(1)} %convolution_bitcast_fusion) | data formatting | bytes 524288 | tf_op jit(solution)/shard_map/transpose | solution.py:450
  7.0 0.1 mul.55
  7.1 0.8 %reshape.150 = f32[8,8,64]{2,1,0:T(8,128)S(1)} reshape(bf16[8,512]{1,0:T(8,128)(2,1)} %param.8) | data formatting | bytes 24576 | tf_op jit(solution)/shard_map/convert_element_type | solution.py:440
  7.9 0.1 copy.32
  8.0 0.1 and_convert_fusion
  8.1 0.7 concatenate.12
  8.8 0.7 copy.35.mask_ref
  9.5 62.3 %shard_map.103 = (bf16[32,12288]{1,0:T(8,128)(2,1)}, f32[32,384]{1,0:T(8,128)}, f32[96,384]{1,0:T(8,128)}) custom-call(f32[64,256]{1,0:T(8,128)} %bitcast.26, f32[16,8,512]{2,1,0:T(8,128)} %bitcast.25, bf16[8,12288]{1,0:T(8,128)(2,1)} %cot_ref.1, f32[8,32]{1,0:T(8,128)} %copy.35.mask_ref, bf16[432,384]{1,0:T(8,128)(2,1)} %win_ref.1, bf16[10368,384]{1,0:T(8,128)(2,1)} %wmid_ref.1), custom_call_target="tpu_custom_call" | custom-call | tf_op jit(solution)/shard_map/pallas_call | solution.py:456
  71.8 0.8 %reshape.148 = f32[12288]{0:T(1024)S(1)} reshape(f32[32,384]{1,0:T(8,128)} %get-tuple-element.7) | data formatting | bytes 98304 | tf_op jit(solution)/shard_map/reshape | solution.py:487
  72.6 0.7 dynamic-slice_multiply_fusion.1
  73.3 0.9 %dynamic-slice_multiply_fusion = f32[81,384]{1,0:T(8,128)S(1)} fusion(f32[96,384]{1,0:T(8,128)} %get-tuple-element.8, s32[]{:T(128)S(6)} %select_n.26), kind=kLoop, calls=%fused_computation.1 | loop fusion | flops 31104 | bytes 248836 | tf_op jit(solution)/shard_map/mul | solution.py:488
  74.2 0.7 mul.68
  74.8 2.1 %copy.41 = bf16[32,12288]{1,0:T(8,128)(2,1)} copy(bf16[32,12288]{1,0:T(8,128)(2,1)} %get-tuple-element.14) | data formatting | bytes 1572864
  (12 shorter events, 0.1 us)

commit v2 on v1

v2 whole, which is shorter than its diff:
```python
import math

import jax
import jax.numpy as jnp
from jax import lax
from jax.experimental import pallas as pl
from jax.experimental.pallas import tpu as pltpu
from jax.sharding import PartitionSpec as P

Z = 16
C = 384
TAPS = 27
TF = 2
TH = 4
TW = 4
CAP = 2
EPS = 1e-06
BF = jnp.bfloat16
F32 = jnp.float32
MESH = pl.DeviceIdType.MESH
ORDERS = (("z", "x", "y"), ("x", "y", "z"), ("y", "z", "x"))
ROWS = 1296
FACTOR = 1.0 / math.sqrt(1024 * TF * TH * TW)
PIECE = 96
GROWS = 80


def al(v, m):
    return pl.multiple_of(v, m)


def kernel(
    ids_ref, fra_ref, hei_ref, wid_ref, lat_ref, cot_ref, win_ref, wmid_ref,
    dec_ref, gin_ref, gmid_ref,
    w, we, snd, rcv, xsf, xsp, xbf, xbp, hf, ub, gb, ru, rg, uef, ut, gyef, gyep, gyes, ghs, df, gif, gib, rgi, gz, gzb,
    rz, gx, gxb, rx, gyv, gyb, ry, g, s1, pa0, pb0, fl0, fr0, pa1, pb1, fl1, fr1, pa2, pb2, fl2, fr2, s2f, s2, f2,
    s3, f3, fm, fg, ud, acc,
    w_sem, a_send, a_recv, c_send, c_recv, r_send, r_recv, d_send, d_recv, i_send, i_recv,
):
    load = lax.axis_index("loader")
    q = lax.axis_index("bucket")
    z, c = load // 2, load % 2
    x, y = q // 4, q % 4
    pos = {"z": z, "x": x, "y": y}
    sib = (z * 2 + (1 - c), q)

    def dev(axis, v):
        if axis == "z":
            return (v * 2 + c, q)
        if axis == "x":
            return (load, v * 4 + y)
        return (load, x * 4 + v)

    def wcopy(i):
        part = pl.ds(i * 1152, 1152)
        return pltpu.make_async_copy(wmid_ref.at[part], w.at[part], w_sem.at[i])

    for i in range(9):
        wcopy(i).start()

    barrier = pltpu.get_barrier_semaphore()

    @pl.loop(1, 16)
    def _(d):
        pl.semaphore_signal(barrier, 1, device_id=(load, lax.rem(q + d, 16)), device_id_type=MESH)

    for d in range(1, 4):
        pl.semaphore_signal(barrier, 1, device_id=dev("z", lax.rem(z + d, 4)), device_id_type=MESH)
    pl.semaphore_signal(barrier, 1, device_id=sib, device_id_type=MESH)

    def iota(shape, dim):
        return lax.broadcasted_iota(jnp.int32, shape, dim)

    def column(ref):
        at, out = iota((8, 1), 0), jnp.zeros((8, 1), jnp.int32)
        for t in range(8):
            out = jnp.where(at == t, ref[t], out)
        return out

    fra, hei, wid = column(fra_ref), column(hei_ref), column(wid_ref)
    lane = iota((8, 512), 1)
    inside = (lane // 256 < fra) & ((lane // 64) % 4 < hei) & ((lane // 16) % 4 < wid)
    xm = jnp.where(inside, lat_ref[...].astype(F32), 0.0)
    edge = jnp.zeros((8, 128), F32)
    xm = jnp.concatenate([edge, xm, edge], axis=1)
    xh = pltpu.roll(xm, 704, 1)
    lane = iota((8, 256), 1)
    for fr in range(8):
        f, r = fr // 4, fr % 4
        win = xm[:, 64 * fr + 64 : 64 * fr + 320] if fr % 2 else xh[:, 64 * fr : 64 * fr + 256]
        keep = lane < 192
        if r == 0:
            keep = keep & (lane >= 64)
        if r == 3:
            keep = keep & (lane < 128)
        ones = (lane >= 192) & (lane - 192 < wid) & (f < fra) & (r < hei)
        xsf[fr * 8 : fr * 8 + 8, :] = jnp.where(keep, win, jnp.where(ones, 1.0, 0.0))
    xs = xsf[...].astype(BF)

    ids = [ids_ref[t] for t in range(8)]
    lane, row = iota((1, 64), 1), iota((256, 64), 0)
    slots = jnp.zeros((1, 64), jnp.int32)
    for t in range(8):
        rank = jnp.int32(0)
        for before in range(t):
            rank += jnp.where(ids[before] == ids[t], 1, 0)
        slots = jnp.where(lane % 8 == t, ids[t] * CAP + rank, slots)
    pick = (row // 16 * 2 + row % 2 == slots) & ((row // 2) % 8 == lane // 8)
    snd[...] = jnp.dot(jnp.where(pick, 1.0, 0.0).astype(BF), xs, preferred_element_type=F32).astype(BF)

    def acopy(d):
        to = lax.rem(q + d, 16)
        return pltpu.make_async_remote_copy(
            snd.at[pl.ds(al(to * 16, 16), 16)], rcv.at[pl.ds(al(q * 16, 16), 16)],
            a_send.at[d], a_recv.at[d], device_id=(load, to), device_id_type=MESH)

    def afrom(d):
        src = lax.rem(q - d + 16, 16)
        rows = pl.ds(al(src * 16, 16), 16)
        return pltpu.make_async_remote_copy(
            snd.at[rows], rcv.at[rows], a_send.at[d], a_recv.at[d], device_id=(load, src), device_id_type=MESH)

    we[...] = jnp.zeros_like(we)
    for a in range(3):
        for b in range(3):
            for cc in range(4):
                for e in range(3):
                    ci = cc + e - 1
                    if 0 <= ci < 4:
                        we[a * 256 + (b * 4 + ci) * 16 : a * 256 + (b * 4 + ci) * 16 + 16, cc * C : cc * C + C] = (
                            win_ref[(a * 9 + b * 3 + e) * 16 : (a * 9 + b * 3 + e) * 16 + 16, :])

    xsp[0:64, :] = jnp.zeros((64, 256), BF)
    xsp[64:128, :] = xs
    h = jnp.dot(xsp[0:64, :], we[0:256, :], preferred_element_type=F32)
    h += jnp.dot(xsp[32:96, :], we[256:512, :], preferred_element_type=F32)
    h += jnp.dot(xsp[64:128, :], we[512:768, :], preferred_element_type=F32)
    for fr in range(8):
        for cc in range(4):
            hf[(fr * 4 + cc) * 8 : (fr * 4 + cc) * 8 + 8, :] = h[fr * 8 : fr * 8 + 8, cc * C : cc * C + C]

    def act(hv):
        rr = lax.rsqrt(jnp.mean(hv * hv, axis=-1, keepdims=True) + EPS)
        gv = hv * rr
        sg = jax.nn.sigmoid(gv)
        return rr, gv, sg

    rr, gn, sg = act(hf[...])
    u = gn * sg
    ub[...] = u.astype(BF)
    cot = cot_ref[...].astype(F32)
    for p in range(32):
        inside = (p // 16 < fra) & ((p // 4) % 4 < hei) & (p % 4 < wid)
        gyef[p * 8 : p * 8 + 8, C : 2 * C] = jnp.where(inside, cot[:, p * C : p * C + C], 0.0)
    gb[...] = gyef[:, C : 2 * C].astype(BF)

    def swap(n):
        src, dst = ((ub, ru), (gb, rg))[n]
        return pltpu.make_async_remote_copy(
            src, dst, c_send.at[n], c_recv.at[n], device_id=sib, device_id_type=MESH)

    pl.semaphore_wait(barrier, 19)
    swap(0).start()
    swap(1).start()

    @pl.loop(1, 16)
    def _(d):
        acopy(d).start()

    own = pl.ds(al(q * 16, 16), 16)
    rcv[own, :] = snd[own, :]

    def spread_u(uv, lanes):
        uef[:, C : 2 * C] = uv
        for fr in range(8):
            lo, hi = slice(fr * 32, fr * 32 + 24), slice(fr * 32 + 8, fr * 32 + 32)
            uef[hi, 0:C] = uef[lo, C : 2 * C]
            uef[lo, 2 * C : 3 * C] = uef[hi, C : 2 * C]
        ut[:, lanes] = uef[...].T.astype(BF)

    uef[...] = jnp.zeros_like(uef)
    spread_u(u, slice(0, 256))
    for fr in range(8):
        lo, hi = slice(fr * 32, fr * 32 + 24), slice(fr * 32 + 8, fr * 32 + 32)
        gyef[lo, 0:C] = gyef[hi, C : 2 * C]
        gyef[fr * 32 + 24 : fr * 32 + 32, 0:C] = jnp.zeros((8, C), F32)
        gyef[hi, 2 * C : 3 * C] = gyef[lo, C : 2 * C]
        gyef[fr * 32 : fr * 32 + 8, 2 * C : 3 * C] = jnp.zeros((8, C), F32)
    gyep[...] = jnp.zeros_like(gyep)
    gyes[...] = jnp.zeros_like(gyes)
    for f in range(2):
        gyep[(f * 6 + 1) * 32 : (f * 6 + 5) * 32, :] = gyef[f * 128 : f * 128 + 128, :].astype(BF)
    swap(0).wait_recv()
    spread_u(ru[...].astype(F32), slice(256, 512))
    swap(1).wait_recv()
    for f in range(2):
        gyes[(f * 6 + 1) * 32 : (f * 6 + 5) * 32, :] = rg[f * 128 : f * 128 + 128, :]

    def shifted(ref, i, lanes):
        a, b = i // 3, i % 3
        o0, o1 = ((2 - a) * 6 + 2 - b) * 32, ((3 - a) * 6 + 2 - b) * 32
        return jnp.concatenate([ref[o0 : o0 + 128, lanes], ref[o1 : o1 + 128, lanes]], axis=0)

    def weight_grad(zz, core):
        first = (zz * 2 + core) * ROWS
        at = first
        while at < first + ROWS:
            i = at // 1152
            lo, hi = at - i * 1152, min(1152, first + ROWS - i * 1152)
            rhs = jnp.concatenate(
                [shifted(gyep, i, slice(C, 2 * C)), shifted(gyes, i, slice(0, C))], axis=0)
            out = jnp.dot(ut[lo:hi, :], rhs, preferred_element_type=F32).astype(BF)
            for j in range(3):
                g[j, zz, at - first : at - first + hi - lo, :] = out[:, j * 128 : j * 128 + 128]
            at += hi - lo

    CUT = 656

    def own1(j, t, h):
        if j == 0:
            return g.at[0, t, CUT * h : (CUT, ROWS)[h]]
        if j == 1:
            return g.at[1, 2 * h : 2 * h + 2, pl.ds(al(320 * t, 16), 336)]
        return s1.at[pl.ds(t * 16 + h * 8, 8)]

    def into(j, side, h):
        ref = ((fl0, fr0), (fl1, fr1), (fl2, fr2))[j][side]
        return ref.at[((0, CUT), (0, 2), (0, 8))[j][h] : ((CUT, ROWS), (2, 4), (8, 16))[j][h]]

    parts = ((pa0, pb0), (pa1, pb1), (pa2, pb2))

    def target(j, n):
        return lax.rem(pos[ORDERS[j][0]] + (2, 2, 1, 3, 1, 3)[n], 4)

    def ring(j, n):
        axis = ORDERS[j][0]
        src, side, dst = (
            (own1(j, target(j, 0), 0), 1, parts[j][0]),
            (own1(j, target(j, 1), 1), 3, parts[j][1]),
            (own1(j, target(j, 2), 1), 1, into(j, 0, 1)),
            (own1(j, target(j, 3), 0), 3, into(j, 1, 0)),
            (parts[j][0], 1, into(j, 0, 0)),
            (parts[j][1], 3, into(j, 1, 1)),
        )[n]
        k = j * 6 + n
        return pltpu.make_async_remote_copy(
            src, dst, r_send.at[k], r_recv.at[k], device_id=dev(axis, lax.rem(pos[axis] + side, 4)),
            device_id_type=MESH)

    def relay():
        for n in range(2):
            for j in range(3):
                ring(j, n).wait_recv()
                ref = parts[j][n]
                ref[...] = ref[...] + own1(j, target(j, 4 + n), n)[...]
                ring(j, 4 + n).start()

    for group in range(2):
        for core in range(2):

            @pl.when(c == core)
            def _():
                weight_grad(group * 2, core)
                weight_grad(group * 2 + 1, core)

        @pl.loop(0, 32)
        def _(k):
            zz, shard = group * 2 + k // 16, lax.rem(k, 16)
            s1[lax.rem(shard, 4) * 16 + zz * 4 + shard // 4] = g[2, zz, pl.ds(al(shard * 80, 16), PIECE), :]

        for n in (0, 3) if group == 0 else (1, 2):
            for j in (2, 1):
                ring(j, n).start()
        for n in range(4):

            @pl.when(target(0, n) // 2 == group)
            def _():
                ring(0, n).start()

    def direct(j, st, d):
        axis = ORDERS[j][st]
        to = lax.rem(pos[axis] + d, 4)
        if st == 1:
            src, dst = s2.at[pl.ds(j * 16 + to * 4, 4)], f2.at[j * 3 + d - 1]
        else:
            src, dst = s3.at[j * 4 + to], f3.at[j * 3 + d - 1]
        k = (st - 1) * 9 + j * 3 + d - 1
        return pltpu.make_async_remote_copy(
            src, dst, d_send.at[k], d_recv.at[k], device_id=dev(axis, to), device_id_type=MESH)

    def second():
        for j in range(3):
            for n in range(2, 6):
                ring(j, n).wait_recv()

            @pl.loop(0, 16)
            def _(k):
                if j == 0:
                    rows = pl.ds(al(k * 80, 16), PIECE)
                    terms = g[0, z, rows, :], fl0[rows, :], fr0[rows, :]
                elif j == 1:
                    yy, zz = k // 4, lax.rem(k, 4)
                    rows = pl.ds(al(yy * 80, 16), PIECE)
                    terms = g[1, zz, pl.ds(al(x * 320 + yy * 80, 16), PIECE), :], fl1[zz, rows, :], fr1[zz, rows, :]
                else:
                    terms = s1[y * 16 + k], fl2[k], fr2[k]
                total = terms[0].astype(F32) + terms[1].astype(F32) + terms[2].astype(F32)
                s2f[j * 16 + k] = total
                s2[j * 16 + k] = total.astype(BF)

            for d in (2, 1, 3):
                direct(j, 1, d).start()

    def third():
        for j in range(3):
            for d in range(1, 4):
                direct(j, 1, d).wait_recv()
            for k in range(4):
                total = s2f[j * 16 + pos[ORDERS[j][1]] * 4 + k]
                for d in range(3):
                    total += f2[j * 3 + d, k].astype(F32)
                s3[j * 4 + k] = total
            for d in (2, 1, 3):
                direct(j, 2, d).start()

    def finish():
        for j in range(3):
            for d in range(1, 4):
                direct(j, 2, d).wait_recv()
            fm[j, 0:PIECE, :] = s3[j * 4 + pos[ORDERS[j][2]]] + f3[j * 3] + f3[j * 3 + 1] + f3[j * 3 + 2]
            fm[j, PIECE:, :] = jnp.zeros((8, 128), F32)
            gmid_ref[pl.ds(j, 88, stride=3), :] = fm[j, pl.ds(q, 88), :] * FACTOR


    for i in range(9):
        wcopy(i).wait()
    gu = jnp.zeros((256, C), F32)
    for i in range(9):
        for e in range(3):
            gu += lax.dot_general(
                shifted(gyep, i, slice(e * C, e * C + C)), w[i * 1152 + e * C : i * 1152 + e * C + C, :],
                (((1,), (1,)), ((), ())), preferred_element_type=F32)

    rr, gn, sg = act(hf[...])
    gv = gu * sg * (1.0 + gn * (1.0 - sg))
    gh = gyef[:, C : 2 * C] + rr * (gv - gn * jnp.mean(gv * gn, axis=-1, keepdims=True))
    hf[...] = gh
    ghs[...] = jnp.zeros_like(ghs)
    for cc in range(4):
        ghs[0:64, cc * C : cc * C + C] = jnp.concatenate(
            [hf[(fr * 4 + cc) * 8 : (fr * 4 + cc) * 8 + 8, :] for fr in range(8)], axis=0).astype(BF)
    xst = xsf[...].T.astype(BF)
    gif[...] = jnp.zeros_like(gif)
    for a in range(3):
        df[...] = jnp.dot(xst, ghs[(2 - a) * 32 : (2 - a) * 32 + 64, :], preferred_element_type=F32)
        for b in range(3):
            for e in range(3):
                total = jnp.zeros((16, C), F32)
                for cc in range(4):
                    ci = cc + e - 1
                    if 0 <= ci < 4:
                        total += df[(b * 4 + ci) * 16 : (b * 4 + ci) * 16 + 16, cc * C : cc * C + C]
                gif[(a * 9 + b * 3 + e) * 16 : (a * 9 + b * 3 + e) * 16 + 16, :] = total
    for blk in range(8):
        at = 16 * ((27 * blk) // 8)
        gib[blk % 2, blk // 2] = gif[at : at + GROWS, :].astype(BF)

    def icore():
        return pltpu.make_async_remote_copy(
            gib.at[1 - c], rgi, i_send.at[0], i_recv.at[0], device_id=sib, device_id_type=MESH)

    base = load * 54 - 16 * ((27 * load) // 8)

    def xstart(v):
        return al(16 * ((2 * base + 27 * v) // 32), 16)

    def ipeer(axis, d):
        v = lax.rem(pos[axis] + d, 4)
        src, dst, k = {
            "z": (gzb.at[v], rz.at[d - 1], 0),
            "x": (gxb.at[pl.ds(xstart(v), 32)], rx.at[d - 1], 3),
            "y": (gyb, ry.at[d - 1], 6),
        }[axis]
        return pltpu.make_async_remote_copy(
            src, dst, i_send.at[k + d], i_recv.at[k + d], device_id=dev(axis, v), device_id_type=MESH)

    def in_z():
        icore().wait_recv()
        for zz in range(4):
            at = al(16 * ((27 * (zz * 2 + c)) // 8), 16)
            total = gif[pl.ds(at, GROWS), :] + rgi[zz].astype(F32)
            gz[zz] = total
            gzb[zz] = total.astype(BF)
        for d in range(1, 4):
            ipeer("z", d).start()

    def in_x():
        for d in range(1, 4):
            ipeer("z", d).wait_recv()
        total = gz[z] + rz[0].astype(F32) + rz[1].astype(F32) + rz[2].astype(F32)
        gx[...] = total
        gxb[...] = total.astype(BF)
        for d in range(1, 4):
            ipeer("x", d).start()

    def in_y():
        for d in range(1, 4):
            ipeer("x", d).wait_recv()
        total = gx[pl.ds(xstart(x), 32), :] + rx[0].astype(F32) + rx[1].astype(F32) + rx[2].astype(F32)
        gyv[...] = total
        gyb[...] = total.astype(BF)
        for d in range(1, 4):
            ipeer("y", d).start()

    def in_end():
        for d in range(1, 4):
            ipeer("y", d).wait_recv()
        total = gyv[...] + ry[0].astype(F32) + ry[1].astype(F32) + ry[2].astype(F32)
        fg[96:, :] = jnp.zeros((8, 128), F32)
        for j in range(3):
            fg[pl.ds(j, 32, stride=3), :] = total[:, j * 128 : j * 128 + 128]
        first = 384 * (base - 16 * ((2 * base + 27 * x) // 32)) + 1296 * q
        at, lo = first // 128, lax.rem(first, 128)
        shift = lax.rem(128 - lo, 128)
        head = pltpu.roll(fg[pl.ds(at, 16), :], shift, 1)
        tail = pltpu.roll(fg[pl.ds(at + 1, 16), :], shift, 1)
        gin_ref[...] = jnp.where(iota((16, 128), 1) < 128 - lo, head, tail) * FACTOR

    icore().start()
    relay()
    in_z()

    @pl.loop(1, 16)
    def _(d):
        afrom(d).wait_recv()

    dst, src = iota((256, 256), 0), iota((256, 256), 1)
    order = (dst // 32 == (src // 2) % 8) & ((dst // 2) % 16 == src // 16) & (dst % 2 == src % 2)
    xbf[...] = jnp.dot(jnp.where(order, 1.0, 0.0).astype(BF), rcv[...], preferred_element_type=F32)
    xbp[0:256, :] = jnp.zeros((256, 256), BF)
    xbp[256:512, :] = xbf[...].astype(BF)
    ud[...] = jnp.zeros_like(ud)
    for f in range(2):
        hd = jnp.dot(xbp[f * 128 : f * 128 + 128, :], we[0:256, :], preferred_element_type=F32)
        hd += jnp.dot(xbp[f * 128 + 128 : f * 128 + 256, :], we[256:512, :], preferred_element_type=F32)
        hd += jnp.dot(xbp[f * 128 + 256 : f * 128 + 384, :], we[512:768, :], preferred_element_type=F32)
        for cc in range(4):
            hc = hd[:, cc * C : cc * C + C]
            _, gc, sc = act(hc)
            uc = (gc * sc).astype(BF)
            for r in range(4):
                rows = slice(r * 32, r * 32 + 32)
                acc[((f * 4 + r) * 4 + cc) * 32 : ((f * 4 + r) * 4 + cc) * 32 + 32, :] = hc[rows]
                to = (f + 2) * 512 + r * 128 + cc * 32
                for e in range(3):
                    if 0 <= cc - e + 1 < 4:
                        ud[to + (1 - e) * 32 : to + (1 - e) * 32 + 32, e * C : e * C + C] = uc[rows]

    def decode(a, f):
        taps = jnp.concatenate([w[(a * 3 + b) * 1152 : (a * 3 + b) * 1152 + 1152, :] for b in range(3)], axis=1)
        out = jnp.dot(ud[(f + a) * 512 : (f + a) * 512 + 512, :], taps, preferred_element_type=F32)
        top = f * 512
        acc[top + 128 : top + 512, :] += out[0:384, 0:C]
        acc[top : top + 512, :] += out[:, C : 2 * C]
        acc[top : top + 384, :] += out[128:512, 2 * C :]

    decode(0, 0)
    decode(0, 1)
    second()
    in_x()
    decode(1, 0)
    decode(1, 1)
    third()
    in_y()
    decode(2, 0)
    decode(2, 1)
    for fr in range(8):
        for cc in range(4):
            p = fr * 4 + cc
            m = xbf[fr * 32 : fr * 32 + 32, 192 + cc : 193 + cc]
            dec_ref[:, p * C : p * C + C] = (acc[p * 32 : p * 32 + 32, :] * m).astype(BF)
    finish()
    in_end()

    @pl.loop(1, 16)
    def _(d):
        acopy(d).wait_send()

    swap(0).wait_send()
    swap(1).wait_send()
    for j in range(3):
        for n in range(6):
            ring(j, n).wait_send()
        for d in range(1, 4):
            direct(j, 1, d).wait_send()
            direct(j, 2, d).wait_send()
    icore().wait_send()
    for axis in ("z", "x", "y"):
        for d in range(1, 4):
            ipeer(axis, d).wait_send()


def shards(latents, cotangent, frames, heights, widths, bucket_ids, w_in, w_mid):
    v = pltpu.VMEM
    dma = pltpu.SemaphoreType.DMA
    vm = pl.BlockSpec(memory_space=pltpu.VMEM)
    sm = pl.BlockSpec(memory_space=pltpu.SMEM)
    dec, gin, gmid = pl.pallas_call(
        kernel,
        out_shape=(
            jax.ShapeDtypeStruct((32, 12288), BF),
            jax.ShapeDtypeStruct((16, 128), F32),
            jax.ShapeDtypeStruct((264, 128), F32),
        ),
        in_specs=[sm, sm, sm, sm, vm, vm, vm, pl.BlockSpec(memory_space=pl.ANY)],
        out_specs=(vm, vm, vm),
        scratch_shapes=[
            v((10368, C), BF), v((768, 1536), BF), v((256, 256), BF), v((256, 256), BF), v((64, 256), F32),
            v((128, 256), BF), v((256, 256), F32), v((512, 256), BF), v((256, C), F32),
            v((256, C), BF), v((256, C), BF), v((256, C), BF), v((256, C), BF), v((256, 1152), F32),
            v((1152, 512), BF), v((256, 1152), F32), v((768, 1152), BF), v((768, C), BF), v((128, 1536), BF),
            v((256, 1536), F32), v((448, C), F32), v((2, 4, GROWS, C), BF), v((4, GROWS, C), BF),
            v((4, GROWS, C), F32), v((4, GROWS, C), BF), v((3, GROWS, C), BF), v((GROWS, C), F32), v((GROWS, C), BF),
            v((3, 32, C), BF), v((32, C), F32), v((32, C), BF), v((3, 32, C), BF), v((3, 4, ROWS, 128), BF),
            v((64, PIECE, 128), BF),
            v((656, 128), BF), v((640, 128), BF), v((ROWS, 128), BF), v((ROWS, 128), BF),
            v((2, 336, 128), BF), v((2, 336, 128), BF), v((4, 336, 128), BF), v((4, 336, 128), BF),
            v((8, PIECE, 128), BF), v((8, PIECE, 128), BF), v((16, PIECE, 128), BF), v((16, PIECE, 128), BF),
            v((48, PIECE, 128), F32), v((48, PIECE, 128), BF), v((9, 4, PIECE, 128), BF), v((12, PIECE, 128), F32),
            v((9, PIECE, 128), F32), v((3, PIECE + 8, 128), F32), v((104, 128), F32), v((2048, 1152), BF),
            v((1024, C), F32),
            dma((9,)), dma((16,)), dma((16,)), dma((2,)), dma((2,)), dma((18,)), dma((18,)), dma((18,)), dma((18,)),
            dma((10,)), dma((10,)),
        ],
        compiler_params=pltpu.CompilerParams(
            collective_id=0, has_side_effects=True, vmem_limit_bytes=62 * 1024 * 1024),
    )(bucket_ids, frames, heights, widths, latents, cotangent, w_in, w_mid)
    return (dec, gin.reshape(-1)[:1296], gmid.reshape(-1)[:31104])


def solution(mesh):
    return jax.shard_map(
        shards,
        mesh=mesh,
        in_specs=(
            P(("loader", "bucket"), None),
            P(("loader", "bucket"), None),
            P(("loader", "bucket")),
            P(("loader", "bucket")),
            P(("loader", "bucket")),
            P(("loader", "bucket")),
            P(),
            P(),
        ),
        out_specs=(P(("loader", "bucket"), None), P(("loader", "bucket")), P(("loader", "bucket"))),
        check_vma=False,
    )
```

time: 77.3 us -> 49.4 us (0.64)
  Pallas kernels: 62.3 us -> 43.5 us
  other arithmetic: 5.29 us -> 0 us
  local copies, waits for them, and re-layouts: 8.27 us -> 4.92 us
    pallas_call x1, Pallas kernels: 62.3 us -> 43.5 us  [shards(): pl.pallas_call(kernel, out_shape=(jax.ShapeDtypeStruct((32, 12288), BF),...]
    convert_element_type x5 -> x0, local copies, waits for them, and re-layouts: 2.48 us -> none  [the longest x2 1.56 us: shards(): xm = latents.reshape(count, TF, TH, TW, Z).astype(F32) * mask[..., None]]
    lt x3 -> x0, other arithmetic: 1.99 us -> none  [the longest x1 0.66 us: tile_mask(): cpos < widths[:, None, None, None]]
    mul x4 -> x0, other arithmetic: 1.63 us -> none  [the longest x1 0.93 us: shards(): grad_mid = lax.dynamic_slice(gmid, (q, 0), (81, C)).reshape(-1) * factor]
    slice x3 -> x1, local copies, waits for them, and re-layouts: 0.04 us -> 1.56 us  [shards(): return (dec, gin.reshape(-1)[:1296], gmid.reshape(-1)[:31104])]
    unnamed x1 -> x2, local copies, waits for them, and re-layouts: 2.06 us -> 3.36 us
    mul x4 -> x0, local copies, waits for them, and re-layouts: 1.02 us -> none  [the longest x1 0.66 us: shards(): grad_mid = lax.dynamic_slice(gmid, (q, 0), (81, C)).reshape(-1) * factor]
    reduce_sum x1 -> x0, other arithmetic: 0.92 us -> none  [shards(): rank = jnp.sum(jnp.tril(same, -1).astype(jnp.int32), axis=1)]
where the time goes in v2:
time: 49.4 us; the launch traced here: 49.1 us
  Pallas kernels  43.5 us (88%)
  local copies, waits for them, and re-layouts  4.92 us (10%)
  between operations  0.64 us (1%)
    pallas_call x1, Pallas kernels, shards(): pl.pallas_call(kernel, out_shape=(jax.ShapeDtypeStruct((32, 12288), BF),...  43.5 us
    unnamed x2, local copies, waits for them, and re-layouts  3.36 us
    slice x1, local copies, waits for them, and re-layouts, shards(): return (dec, gin.reshape(-1)[:1296], gmid.reshape(-1)[:31104])  1.56 us

profile of v2, /device:TPU:0, one launch (start us, length us, event | category | flops | bytes accessed | tf_op | source)
XLA Modules:
  0.0 49.1 jit_solution(15703841730421272501)
XLA Ops:
  0.6 43.5 %shard_map.103 = (bf16[32,12288]{1,0:T(8,128)(2,1)}, f32[16,128]{1,0:T(8,128)}, f32[264,128]{1,0:T(8,128)}) custom-call(s32[8]{0:T(128)} %ids_ref.1, s32[8]{0:T(128)} %fra_ref.1, s32[8]{0:T(128)} %hei_ref.1, s32[8]{0:T(128)} %wid_ref.1, bf16[8,512]{1,0:T(8,128)(2,1)} %lat_ref.1, bf16[8,12288]{1,0:T(8,128)(2,1)} %cot_ref.1, bf16[432,384]{1,0:T(8,128)(2,1)} %win_ref.1, ...), custom_call_target="tpu_custom_call" | custom-call | tf_op jit(solution)/shard_map/pallas_call | solution.py:508
  44.2 1.6 %slice_bitcast_fusion = f32[31104]{0:T(1024)} fusion(f32[264,128]{1,0:T(8,128)} %get-tuple-element.8), kind=kLoop, calls=%fused_computation | loop fusion | bytes 248832 | tf_op jit(solution)/shard_map/slice | solution.py:538
  45.7 2.1 %copy.13 = bf16[32,12288]{1,0:T(8,128)(2,1)} copy(bf16[32,12288]{1,0:T(8,128)(2,1)} %get-tuple-element.12) | data formatting | bytes 1572864
  47.8 1.3 %copy.14 = f32[1296]{0:T(1024)} copy(f32[1296]{0:T(1024)} %bitcast.4) | data formatting | bytes 10368

commit v3 on v2

--- a/solution.py
+++ b/solution.py
@@ -30,12 +30,12 @@
 
 
 def kernel(
-    ids_ref, fra_ref, hei_ref, wid_ref, lat_ref, cot_ref, win_ref, wmid_ref,
-    dec_ref, gin_ref, gmid_ref,
+    ids_ref, fra_ref, hei_ref, wid_ref, lat_hbm, cot_hbm, win_hbm, wmid_ref,
+    dec_hbm, gin_ref, gmid_ref,
     w, we, snd, rcv, xsf, xsp, xbf, xbp, hf, ub, gb, ru, rg, uef, ut, gyef, gyep, gyes, ghs, df, gif, gib, rgi, gz, gzb,
     rz, gx, gxb, rx, gyv, gyb, ry, g, s1, pa0, pb0, fl0, fr0, pa1, pb1, fl1, fr1, pa2, pb2, fl2, fr2, s2f, s2, f2,
-    s3, f3, fm, fg, ud, acc,
-    w_sem, a_send, a_recv, c_send, c_recv, r_send, r_recv, d_send, d_recv, i_send, i_recv,
+    s3, f3, fm, fo, fg, ud, acc, lat_ref, cot_ref, win_ref, dec_ref,
+    o_sem, w_sem, a_send, a_recv, c_send, c_recv, r_send, r_recv, d_send, d_recv, i_send, i_recv,
 ):
     load = lax.axis_index("loader")
     q = lax.axis_index("bucket")
@@ -55,8 +55,18 @@
         part = pl.ds(i * 1152, 1152)
         return pltpu.make_async_copy(wmid_ref.at[part], w.at[part], w_sem.at[i])
 
+    loads = [
+        pltpu.make_async_copy(src, dst, o_sem.at[n])
+        for n, (src, dst) in enumerate(((lat_hbm, lat_ref), (win_hbm, win_ref), (cot_hbm, cot_ref)))
+    ]
+    for load_in in loads:
+        load_in.start()
     for i in range(9):
         wcopy(i).start()
+
+    def store(f):
+        lanes = slice(f * 6144, f * 6144 + 6144)
+        return pltpu.make_async_copy(dec_ref.at[:, lanes], dec_hbm.at[:, lanes], o_sem.at[3 + f])
 
     barrier = pltpu.get_barrier_semaphore()
 
@@ -77,6 +87,7 @@
             out = jnp.where(at == t, ref[t], out)
         return out
 
+    loads[0].wait()
     fra, hei, wid = column(fra_ref), column(hei_ref), column(wid_ref)
     lane = iota((8, 512), 1)
     inside = (lane // 256 < fra) & ((lane // 64) % 4 < hei) & ((lane // 16) % 4 < wid)
@@ -97,6 +108,63 @@
         xsf[fr * 8 : fr * 8 + 8, :] = jnp.where(keep, win, jnp.where(ones, 1.0, 0.0))
     xs = xsf[...].astype(BF)
 
+    def acopy(d):
+        to = lax.rem(q + d, 16)
+        return pltpu.make_async_remote_copy(
+            snd.at[pl.ds(al(to * 16, 16), 16)], rcv.at[pl.ds(al(q * 16, 16), 16)],
+            a_send.at[d], a_recv.at[d], device_id=(load, to), device_id_type=MESH)
+
+    def afrom(d):
+        src = lax.rem(q - d + 16, 16)
+        rows = pl.ds(al(src * 16, 16), 16)
+        return pltpu.make_async_remote_copy(
+            snd.at[rows], rcv.at[rows], a_send.at[d], a_recv.at[d], device_id=(load, src), device_id_type=MESH)
+
+    we[...] = jnp.zeros_like(we)
+    loads[1].wait()
+    for a in range(3):
+        for b in range(3):
+            for cc in range(4):
+                for e in range(3):
+                    ci = cc + e - 1
+                    if 0 <= ci < 4:
+                        we[a * 256 + (b * 4 + ci) * 16 : a * 256 + (b * 4 + ci) * 16 + 16, cc * C : cc * C + C] = (
+                            win_ref[(a * 9 + b * 3 + e) * 16 : (a * 9 + b * 3 + e) * 16 + 16, :])
+
+    xsp[0:64, :] = jnp.zeros((64, 256), BF)
+    xsp[64:128, :] = xs
+    h = jnp.dot(xsp[0:64, :], we[0:256, :], preferred_element_type=F32)
+    h += jnp.dot(xsp[32:96, :], we[256:512, :], preferred_element_type=F32)
+    h += jnp.dot(xsp[64:128, :], we[512:768, :], preferred_element_type=F32)
+    for fr in range(8):
+        for cc in range(4):
+            hf[(fr * 4 + cc) * 8 : (fr * 4 + cc) * 8 + 8, :] = h[fr * 8 : fr * 8 + 8, cc * C : cc * C + C]
+
+    def act(hv):
+        rr = lax.rsqrt(jnp.mean(hv * hv, axis=-1, keepdims=True) + EPS)
+        gv = hv * rr
+        sg = jax.nn.sigmoid(gv)
+        return rr, gv, sg
+
+    rr, gn, sg = act(hf[...])
+    u = gn * sg
+    ub[...] = u.astype(BF)
+    loads[2].wait()
+    cot = cot_ref[...].astype(F32)
+    for p in range(32):
+        inside = (p // 16 < fra) & ((p // 4) % 4 < hei) & (p % 4 < wid)
+        gyef[p * 8 : p * 8 + 8, C : 2 * C] = jnp.where(inside, cot[:, p * C : p * C + C], 0.0)
+    gb[...] = gyef[:, C : 2 * C].astype(BF)
+
+    def swap(n):
+        src, dst = ((ub, ru), (gb, rg))[n]
+        return pltpu.make_async_remote_copy(
+            src, dst, c_send.at[n], c_recv.at[n], device_id=sib, device_id_type=MESH)
+
+    pl.semaphore_wait(barrier, 19)
+    swap(0).start()
+    swap(1).start()
+
     ids = [ids_ref[t] for t in range(8)]
     lane, row = iota((1, 64), 1), iota((256, 64), 0)
     slots = jnp.zeros((1, 64), jnp.int32)
@@ -107,61 +175,6 @@
         slots = jnp.where(lane % 8 == t, ids[t] * CAP + rank, slots)
     pick = (row // 16 * 2 + row % 2 == slots) & ((row // 2) % 8 == lane // 8)
     snd[...] = jnp.dot(jnp.where(pick, 1.0, 0.0).astype(BF), xs, preferred_element_type=F32).astype(BF)
-
-    def acopy(d):
-        to = lax.rem(q + d, 16)
-        return pltpu.make_async_remote_copy(
-            snd.at[pl.ds(al(to * 16, 16), 16)], rcv.at[pl.ds(al(q * 16, 16), 16)],
-            a_send.at[d], a_recv.at[d], device_id=(load, to), device_id_type=MESH)
-
-    def afrom(d):
-        src = lax.rem(q - d + 16, 16)
-        rows = pl.ds(al(src * 16, 16), 16)
-        return pltpu.make_async_remote_copy(
-            snd.at[rows], rcv.at[rows], a_send.at[d], a_recv.at[d], device_id=(load, src), device_id_type=MESH)
-
-    we[...] = jnp.zeros_like(we)
-    for a in range(3):
-        for b in range(3):
-            for cc in range(4):
-                for e in range(3):
-                    ci = cc + e - 1
-                    if 0 <= ci < 4:
-                        we[a * 256 + (b * 4 + ci) * 16 : a * 256 + (b * 4 + ci) * 16 + 16, cc * C : cc * C + C] = (
-                            win_ref[(a * 9 + b * 3 + e) * 16 : (a * 9 + b * 3 + e) * 16 + 16, :])
-
-    xsp[0:64, :] = jnp.zeros((64, 256), BF)
-    xsp[64:128, :] = xs
-    h = jnp.dot(xsp[0:64, :], we[0:256, :], preferred_element_type=F32)
-    h += jnp.dot(xsp[32:96, :], we[256:512, :], preferred_element_type=F32)
-    h += jnp.dot(xsp[64:128, :], we[512:768, :], preferred_element_type=F32)
-    for fr in range(8):
-        for cc in range(4):
-            hf[(fr * 4 + cc) * 8 : (fr * 4 + cc) * 8 + 8, :] = h[fr * 8 : fr * 8 + 8, cc * C : cc * C + C]
-
-    def act(hv):
-        rr = lax.rsqrt(jnp.mean(hv * hv, axis=-1, keepdims=True) + EPS)
-        gv = hv * rr
-        sg = jax.nn.sigmoid(gv)
-        return rr, gv, sg
-
-    rr, gn, sg = act(hf[...])
-    u = gn * sg
-    ub[...] = u.astype(BF)
-    cot = cot_ref[...].astype(F32)
-    for p in range(32):
-        inside = (p // 16 < fra) & ((p // 4) % 4 < hei) & (p % 4 < wid)
-        gyef[p * 8 : p * 8 + 8, C : 2 * C] = jnp.where(inside, cot[:, p * C : p * C + C], 0.0)
-    gb[...] = gyef[:, C : 2 * C].astype(BF)
-
-    def swap(n):
-        src, dst = ((ub, ru), (gb, rg))[n]
-        return pltpu.make_async_remote_copy(
-            src, dst, c_send.at[n], c_recv.at[n], device_id=sib, device_id_type=MESH)
-
-    pl.semaphore_wait(barrier, 19)
-    swap(0).start()
-    swap(1).start()
 
     @pl.loop(1, 16)
     def _(d):
@@ -215,45 +228,54 @@
             at += hi - lo
 
     CUT = 656
-
-    def own1(j, t, h):
+    PIECES = (1, 2, 2)
+
+    def own1(j, t, h, r):
         if j == 0:
             return g.at[0, t, CUT * h : (CUT, ROWS)[h]]
         if j == 1:
-            return g.at[1, 2 * h : 2 * h + 2, pl.ds(al(320 * t, 16), 336)]
-        return s1.at[pl.ds(t * 16 + h * 8, 8)]
-
-    def into(j, side, h):
+            return g.at[1, 2 * r + h, pl.ds(al(320 * t, 16), 336)]
+        return s1.at[pl.ds(t * 16 + (2 * r + h) * 4, 4)]
+
+    def into(j, side, h, r):
         ref = ((fl0, fr0), (fl1, fr1), (fl2, fr2))[j][side]
-        return ref.at[((0, CUT), (0, 2), (0, 8))[j][h] : ((CUT, ROWS), (2, 4), (8, 16))[j][h]]
-
-    parts = ((pa0, pb0), (pa1, pb1), (pa2, pb2))
+        if j == 0:
+            return ref.at[CUT * h : (CUT, ROWS)[h]]
+        if j == 1:
+            return ref.at[2 * r + h]
+        return ref.at[(2 * r + h) * 4 : (2 * r + h) * 4 + 4]
+
+    def part(j, h, r):
+        ref = ((pa0, pb0), (pa1, pb1), (pa2, pb2))[j][h]
+        if j == 0:
+            return ref
+        return ref.at[r] if j == 1 else ref.at[r * 4 : r * 4 + 4]
 
     def target(j, n):
         return lax.rem(pos[ORDERS[j][0]] + (2, 2, 1, 3, 1, 3)[n], 4)
 
-    def ring(j, n):
+    def ring(j, n, r):
         axis = ORDERS[j][0]
         src, side, dst = (
-            (own1(j, target(j, 0), 0), 1, parts[j][0]),
-            (own1(j, target(j, 1), 1), 3, parts[j][1]),
-            (own1(j, target(j, 2), 1), 1, into(j, 0, 1)),
-            (own1(j, target(j, 3), 0), 3, into(j, 1, 0)),
-            (parts[j][0], 1, into(j, 0, 0)),
-            (parts[j][1], 3, into(j, 1, 1)),
+            (own1(j, target(j, 0), 0, r), 1, part(j, 0, r)),
+            (own1(j, target(j, 1), 1, r), 3, part(j, 1, r)),
+            (own1(j, target(j, 2), 1, r), 1, into(j, 0, 1, r)),
+            (own1(j, target(j, 3), 0, r), 3, into(j, 1, 0, r)),
+            (part(j, 0, r), 1, into(j, 0, 0, r)),
+            (part(j, 1, r), 3, into(j, 1, 1, r)),
         )[n]
-        k = j * 6 + n
+        k = (j * 6 + n) * 2 + r
         return pltpu.make_async_remote_copy(
             src, dst, r_send.at[k], r_recv.at[k], device_id=dev(axis, lax.rem(pos[axis] + side, 4)),
             device_id_type=MESH)
 
     def relay():
-        for n in range(2):
-            for j in range(3):
-                ring(j, n).wait_recv()
-                ref = parts[j][n]
-                ref[...] = ref[...] + own1(j, target(j, 4 + n), n)[...]
-                ring(j, 4 + n).start()
+        for j, r in ((1, 0), (2, 0), (0, 0), (1, 1), (2, 1)):
+            for n in range(2):
+                ring(j, n, r).wait_recv()
+                ref = part(j, n, r)
+                ref[...] = ref[...] + own1(j, target(j, 4 + n), n, r)[...]
+                ring(j, 4 + n, r).start()
 
     for group in range(2):
         for core in range(2):
@@ -268,14 +290,14 @@
             zz, shard = group * 2 + k // 16, lax.rem(k, 16)
             s1[lax.rem(shard, 4) * 16 + zz * 4 + shard // 4] = g[2, zz, pl.ds(al(shard * 80, 16), PIECE), :]
 
-        for n in (0, 3) if group == 0 else (1, 2):
+        for n in range(4):
             for j in (2, 1):
-                ring(j, n).start()
+                ring(j, n, group).start()
         for n in range(4):
 
             @pl.when(target(0, n) // 2 == group)
             def _():
-                ring(0, n).start()
+                ring(0, n, 0).start()
 
     def direct(j, st, d):
         axis = ORDERS[j][st]
@@ -291,7 +313,8 @@
     def second():
         for j in range(3):
             for n in range(2, 6):
-                ring(j, n).wait_recv()
+                for r in range(PIECES[j]):
+                    ring(j, n, r).wait_recv()
 
             @pl.loop(0, 16)
             def _(k):
@@ -329,7 +352,8 @@
                 direct(j, 2, d).wait_recv()
             fm[j, 0:PIECE, :] = s3[j * 4 + pos[ORDERS[j][2]]] + f3[j * 3] + f3[j * 3 + 1] + f3[j * 3 + 2]
             fm[j, PIECE:, :] = jnp.zeros((8, 128), F32)
-            gmid_ref[pl.ds(j, 88, stride=3), :] = fm[j, pl.ds(q, 88), :] * FACTOR
+            fo[pl.ds(j, 88, stride=3), :] = fm[j, pl.ds(q, 88), :]
+        gmid_ref[...] = fo[0:243, :]
 
 
     for i in range(9):
@@ -424,7 +448,7 @@
         shift = lax.rem(128 - lo, 128)
         head = pltpu.roll(fg[pl.ds(at, 16), :], shift, 1)
         tail = pltpu.roll(fg[pl.ds(at + 1, 16), :], shift, 1)
-        gin_ref[...] = jnp.where(iota((16, 128), 1) < 128 - lo, head, tail) * FACTOR
+        gin_ref[...] = jnp.where(iota((16, 128), 1) < 128 - lo, head, tail)
 
     icore().start()
     relay()
@@ -464,6 +488,12 @@
         acc[top : top + 512, :] += out[:, C : 2 * C]
         acc[top : top + 384, :] += out[128:512, 2 * C :]
 
+    def emit(f):
+        for p in range(16 * f, 16 * f + 16):
+            m = xbf[p // 4 * 32 : p // 4 * 32 + 32, 192 + p % 4 : 193 + p % 4]
+            dec_ref[:, p * C : p * C + C] = (acc[p * 32 : p * 32 + 32, :] * m).astype(BF)
+        store(f).start()
+
     decode(0, 0)
     decode(0, 1)
     second()
@@ -473,12 +503,9 @@
     third()
     in_y()
     decode(2, 0)
+    emit(0)
     decode(2, 1)
-    for fr in range(8):
-        for cc in range(4):
-            p = fr * 4 + cc
-            m = xbf[fr * 32 : fr * 32 + 32, 192 + cc : 193 + cc]
-            dec_ref[:, p * C : p * C + C] = (acc[p * 32 : p * 32 + 32, :] * m).astype(BF)
+    emit(1)
     finish()
     in_end()
 
@@ -486,11 +513,14 @@
     def _(d):
         acopy(d).wait_send()
 
+    store(0).wait()
+    store(1).wait()
     swap(0).wait_send()
     swap(1).wait_send()
     for j in range(3):
         for n in range(6):
-            ring(j, n).wait_send()
+            for r in range(PIECES[j]):
+                ring(j, n, r).wait_send()
         for d in range(1, 4):
             direct(j, 1, d).wait_send()
             direct(j, 2, d).wait_send()
@@ -498,6 +528,28 @@
     for axis in ("z", "x", "y"):
         for d in range(1, 4):
             ipeer(axis, d).wait_send()
+
+
+def deliver(d_ref, i_ref, m_ref, dec_ref, gin_ref, gmid_ref, d_buf, i_buf, m_buf, sem):
+    ins = [pltpu.make_async_copy(a, b, sem.at[n]) for n, (a, b) in enumerate(
+        ((i_ref, i_buf), (m_ref, m_buf), (d_ref.at[:, 0:6144], d_buf.at[:, 0:6144]),
+         (d_ref.at[:, 6144:], d_buf.at[:, 6144:])))]
+    for copy in ins:
+        copy.start()
+    ins[0].wait()
+    for n in range(10):
+        gin_ref[pl.ds(n * 128, 128)] = i_buf[n, :] * FACTOR
+    gin_ref[pl.ds(1280, 16)] = i_buf[10, 0:16] * FACTOR
+    ins[1].wait()
+    m_buf[...] = m_buf[...] * FACTOR
+    outs = [pltpu.make_async_copy(a, b, sem.at[4 + n]) for n, (a, b) in enumerate(
+        ((m_buf, gmid_ref), (d_buf.at[:, 0:6144], dec_ref.at[:, 0:6144]), (d_buf.at[:, 6144:], dec_ref.at[:, 6144:])))]
+    outs[0].start()
+    for n in (1, 2):
+        ins[n + 1].wait()
+        outs[n].start()
+    for copy in outs:
+        copy.wait()
 
 
 def shards(latents, cotangent, frames, heights, widths, bucket_ids, w_in, w_mid):
@@ -505,15 +557,16 @@
     dma = pltpu.SemaphoreType.DMA
     vm = pl.BlockSpec(memory_space=pltpu.VMEM)
     sm = pl.BlockSpec(memory_space=pltpu.SMEM)
+    hbm = pl.BlockSpec(memory_space=pl.ANY)
     dec, gin, gmid = pl.pallas_call(
         kernel,
         out_shape=(
             jax.ShapeDtypeStruct((32, 12288), BF),
             jax.ShapeDtypeStruct((16, 128), F32),
-            jax.ShapeDtypeStruct((264, 128), F32),
+            jax.ShapeDtypeStruct((243, 128), F32),
         ),
-        in_specs=[sm, sm, sm, sm, vm, vm, vm, pl.BlockSpec(memory_space=pl.ANY)],
-        out_specs=(vm, vm, vm),
+        in_specs=[sm, sm, sm, sm, hbm, hbm, hbm, hbm],
+        out_specs=(hbm, vm, vm),
         scratch_shapes=[
             v((10368, C), BF), v((768, 1536), BF), v((256, 256), BF), v((256, 256), BF), v((64, 256), F32),
             v((128, 256), BF), v((256, 256), F32), v((512, 256), BF), v((256, C), F32),
@@ -527,15 +580,26 @@
             v((2, 336, 128), BF), v((2, 336, 128), BF), v((4, 336, 128), BF), v((4, 336, 128), BF),
             v((8, PIECE, 128), BF), v((8, PIECE, 128), BF), v((16, PIECE, 128), BF), v((16, PIECE, 128), BF),
             v((48, PIECE, 128), F32), v((48, PIECE, 128), BF), v((9, 4, PIECE, 128), BF), v((12, PIECE, 128), F32),
-            v((9, PIECE, 128), F32), v((3, PIECE + 8, 128), F32), v((104, 128), F32), v((2048, 1152), BF),
-            v((1024, C), F32),
-            dma((9,)), dma((16,)), dma((16,)), dma((2,)), dma((2,)), dma((18,)), dma((18,)), dma((18,)), dma((18,)),
+            v((9, PIECE, 128), F32), v((3, PIECE + 8, 128), F32), v((264, 128), F32), v((104, 128), F32),
+            v((2048, 1152), BF), v((1024, C), F32), v((8, 512), BF), v((8, 12288), BF), v((432, C), BF), v((32, 12288), BF),
+            dma((5,)), dma((9,)), dma((16,)), dma((16,)), dma((2,)), dma((2,)), dma((36,)), dma((36,)), dma((18,)), dma((18,)),
             dma((10,)), dma((10,)),
         ],
         compiler_params=pltpu.CompilerParams(
             collective_id=0, has_side_effects=True, vmem_limit_bytes=62 * 1024 * 1024),
     )(bucket_ids, frames, heights, widths, latents, cotangent, w_in, w_mid)
-    return (dec, gin.reshape(-1)[:1296], gmid.reshape(-1)[:31104])
+    dec, gin, gmid = pl.pallas_call(
+        deliver,
+        out_shape=(
+            jax.ShapeDtypeStruct((32, 12288), BF),
+            jax.ShapeDtypeStruct((1296,), F32),
+            jax.ShapeDtypeStruct((243, 128), F32),
+        ),
+        in_specs=[hbm, hbm, hbm],
+        out_specs=(hbm, vm, hbm),
+        scratch_shapes=[v((32, 12288), BF), v((16, 128), F32), v((243, 128), F32), dma((7,))],
+    )(dec, gin, gmid)
+    return (dec, gin, gmid.reshape(-1))
 
 
 def solution(mesh):

time: 49.4 us -> 46.5 us (0.941)
  local copies, waits for them, and re-layouts: 4.92 us -> 0 us
  Pallas kernels: 43.5 us -> 45.1 us
    unnamed x2 -> x0, local copies, waits for them, and re-layouts: 3.36 us -> none
    pallas_call x0 -> x1, Pallas kernels: none -> 2.61 us  [shards(): pl.pallas_call(deliver, out_shape=(jax.ShapeDtypeStruct((32, 12288), BF),...]
    slice x1 -> x0, local copies, waits for them, and re-layouts: 1.56 us -> none  [shards(): return (dec, gin.reshape(-1)[:1296], gmid.reshape(-1)[:31104])]
    pallas_call x1, Pallas kernels: 43.5 us -> 42.5 us  [shards(): pl.pallas_call(kernel, out_shape=(jax.ShapeDtypeStruct((32, 12288), BF),...]
where the time goes in v3:
time: 46.5 us; the launch traced here: 45.9 us
  Pallas kernels  45.1 us (97%)
  between operations  0.82 us (2%)
    pallas_call x1, Pallas kernels, shards(): pl.pallas_call(kernel, out_shape=(jax.ShapeDtypeStruct((32, 12288), BF),...  42.5 us
    pallas_call x1, Pallas kernels, shards(): pl.pallas_call(deliver, out_shape=(jax.ShapeDtypeStruct((32, 12288), BF),...  2.61 us

profile of v3, /device:TPU:0, one launch (start us, length us, event | category | flops | bytes accessed | tf_op | source)
XLA Modules:
  0.0 45.9 jit_solution(15606276304909704600)
XLA Ops:
  0.6 42.5 %shard_map.103 = (bf16[32,12288]{1,0:T(8,128)(2,1)}, f32[16,128]{1,0:T(8,128)}, f32[243,128]{1,0:T(8,128)}) custom-call(s32[8]{0:T(128)} %ids_ref.1, s32[8]{0:T(128)} %fra_ref.1, s32[8]{0:T(128)} %hei_ref.1, s32[8]{0:T(128)} %wid_ref.1, bf16[8,512]{1,0:T(8,128)(2,1)} %lat_hbm.1, bf16[8,12288]{1,0:T(8,128)(2,1)} %cot_hbm.1, bf16[432,384]{1,0:T(8,128)(2,1)} %win_hbm.1, ...), custom_call_target="tpu_custom_call" | custom-call | tf_op jit(solution)/shard_map/pallas_call | solution.py:561
  43.1 2.6 %shard_map.104 = (bf16[32,12288]{1,0:T(8,128)(2,1)}, f32[1296]{0:T(1024)}, f32[243,128]{1,0:T(8,128)}) custom-call(bf16[32,12288]{1,0:T(8,128)(2,1)} %get-tuple-element.9.d_ref, f32[16,128]{1,0:T(8,128)} %get-tuple-element.10.i_ref, f32[243,128]{1,0:T(8,128)} %get-tuple-element.11.m_ref), custom_call_target="tpu_custom_call" | custom-call | tf_op jit(solution)/shard_map/pallas_call | solution.py:591

commit v4 on v3

--- a/solution.py
+++ b/solution.py
@@ -365,6 +365,7 @@
                 shifted(gyep, i, slice(e * C, e * C + C)), w[i * 1152 + e * C : i * 1152 + e * C + C, :],
                 (((1,), (1,)), ((), ())), preferred_element_type=F32)
 
+    relay()
     rr, gn, sg = act(hf[...])
     gv = gu * sg * (1.0 + gn * (1.0 - sg))
     gh = gyef[:, C : 2 * C] + rr * (gv - gn * jnp.mean(gv * gn, axis=-1, keepdims=True))
@@ -451,7 +452,6 @@
         gin_ref[...] = jnp.where(iota((16, 128), 1) < 128 - lo, head, tail)
 
     icore().start()
-    relay()
     in_z()
 
     @pl.loop(1, 16)

time: 46.5 us -> 48.7 us (1.047)
  Pallas kernels: 45.1 us -> 47 us
    pallas_call x1, Pallas kernels: 42.5 us -> 44.4 us  [shards(): pl.pallas_call(kernel, out_shape=(jax.ShapeDtypeStruct((32, 12288), BF),...]
where the time goes in v4:
time: 48.7 us; the launch traced here: 47.8 us
  Pallas kernels  47 us (97%)
  between operations  0.82 us (2%)
    pallas_call x1, Pallas kernels, shards(): pl.pallas_call(kernel, out_shape=(jax.ShapeDtypeStruct((32, 12288), BF),...  44.4 us
    pallas_call x1, Pallas kernels, shards(): pl.pallas_call(deliver, out_shape=(jax.ShapeDtypeStruct((32, 12288), BF),...  2.61 us

profile of v4, /device:TPU:0, one launch (start us, length us, event | category | flops | bytes accessed | tf_op | source)
XLA Modules:
  0.0 47.8 jit_solution(5908658887738433312)
XLA Ops:
  0.6 44.4 %shard_map.103 = (bf16[32,12288]{1,0:T(8,128)(2,1)}, f32[16,128]{1,0:T(8,128)}, f32[243,128]{1,0:T(8,128)}) custom-call(s32[8]{0:T(128)} %ids_ref.1, s32[8]{0:T(128)} %fra_ref.1, s32[8]{0:T(128)} %hei_ref.1, s32[8]{0:T(128)} %wid_ref.1, bf16[8,512]{1,0:T(8,128)(2,1)} %lat_hbm.1, bf16[8,12288]{1,0:T(8,128)(2,1)} %cot_hbm.1, bf16[432,384]{1,0:T(8,128)(2,1)} %win_hbm.1, ...), custom_call_target="tpu_custom_call" | custom-call | tf_op jit(solution)/shard_map/pallas_call | solution.py:561
  45.0 2.6 %shard_map.104 = (bf16[32,12288]{1,0:T(8,128)(2,1)}, f32[1296]{0:T(1024)}, f32[243,128]{1,0:T(8,128)}) custom-call(bf16[32,12288]{1,0:T(8,128)(2,1)} %get-tuple-element.9.d_ref, f32[16,128]{1,0:T(8,128)} %get-tuple-element.10.i_ref, f32[243,128]{1,0:T(8,128)} %get-tuple-element.11.m_ref), custom_call_target="tpu_custom_call" | custom-call | tf_op jit(solution)/shard_map/pallas_call | solution.py:591

commit v5 on v4

--- a/solution.py
+++ b/solution.py
@@ -269,8 +269,8 @@
             src, dst, r_send.at[k], r_recv.at[k], device_id=dev(axis, lax.rem(pos[axis] + side, 4)),
             device_id_type=MESH)
 
-    def relay():
-        for j, r in ((1, 0), (2, 0), (0, 0), (1, 1), (2, 1)):
+    def relay(pieces):
+        for j, r in pieces:
             for n in range(2):
                 ring(j, n, r).wait_recv()
                 ref = part(j, n, r)
@@ -365,7 +365,6 @@
                 shifted(gyep, i, slice(e * C, e * C + C)), w[i * 1152 + e * C : i * 1152 + e * C + C, :],
                 (((1,), (1,)), ((), ())), preferred_element_type=F32)
 
-    relay()
     rr, gn, sg = act(hf[...])
     gv = gu * sg * (1.0 + gn * (1.0 - sg))
     gh = gyef[:, C : 2 * C] + rr * (gv - gn * jnp.mean(gv * gn, axis=-1, keepdims=True))
@@ -452,7 +451,7 @@
         gin_ref[...] = jnp.where(iota((16, 128), 1) < 128 - lo, head, tail)
 
     icore().start()
-    in_z()
+    relay(((1, 0), (2, 0)))
 
     @pl.loop(1, 16)
     def _(d):
@@ -479,6 +478,9 @@
                 for e in range(3):
                     if 0 <= cc - e + 1 < 4:
                         ud[to + (1 - e) * 32 : to + (1 - e) * 32 + 32, e * C : e * C + C] = uc[rows]
+
+    relay(((0, 0), (1, 1), (2, 1)))
+    in_z()
 
     def decode(a, f):
         taps = jnp.concatenate([w[(a * 3 + b) * 1152 : (a * 3 + b) * 1152 + 1152, :] for b in range(3)], axis=1)

time: 48.7 us -> 46.9 us (0.963); the launches traced: 47.8 us -> 46.7 us
  Pallas kernels: 47 us -> 45.9 us
    pallas_call x1, Pallas kernels: 44.4 us -> 43.3 us  [shards(): pl.pallas_call(kernel, out_shape=(jax.ShapeDtypeStruct((32, 12288), BF),...]
where the time goes in v5:
time: 46.9 us; the launch traced here: 46.7 us
  Pallas kernels  45.9 us (98%)
  between operations  0.82 us (2%)
    pallas_call x1, Pallas kernels, shards(): pl.pallas_call(kernel, out_shape=(jax.ShapeDtypeStruct((32, 12288), BF),...  43.3 us
    pallas_call x1, Pallas kernels, shards(): pl.pallas_call(deliver, out_shape=(jax.ShapeDtypeStruct((32, 12288), BF),...  2.61 us

profile of v5, /device:TPU:0, one launch (start us, length us, event | category | flops | bytes accessed | tf_op | source)
XLA Modules:
  0.0 46.7 jit_solution(4851385858467132487)
XLA Ops:
  0.6 43.3 %shard_map.103 = (bf16[32,12288]{1,0:T(8,128)(2,1)}, f32[16,128]{1,0:T(8,128)}, f32[243,128]{1,0:T(8,128)}) custom-call(s32[8]{0:T(128)} %ids_ref.1, s32[8]{0:T(128)} %fra_ref.1, s32[8]{0:T(128)} %hei_ref.1, s32[8]{0:T(128)} %wid_ref.1, bf16[8,512]{1,0:T(8,128)(2,1)} %lat_hbm.1, bf16[8,12288]{1,0:T(8,128)(2,1)} %cot_hbm.1, bf16[432,384]{1,0:T(8,128)(2,1)} %win_hbm.1, ...), custom_call_target="tpu_custom_call" | custom-call | tf_op jit(solution)/shard_map/pallas_call | solution.py:563
  43.9 2.6 %shard_map.104 = (bf16[32,12288]{1,0:T(8,128)(2,1)}, f32[1296]{0:T(1024)}, f32[243,128]{1,0:T(8,128)}) custom-call(bf16[32,12288]{1,0:T(8,128)(2,1)} %get-tuple-element.9.d_ref, f32[16,128]{1,0:T(8,128)} %get-tuple-element.10.i_ref, f32[243,128]{1,0:T(8,128)} %get-tuple-element.11.m_ref), custom_call_target="tpu_custom_call" | custom-call | tf_op jit(solution)/shard_map/pallas_call | solution.py:593
